TPU v7x, 32 devices: a whole 2x2x4 slice. The times are simulated.
32 devices in a mesh: src: 4 (over z), rcv: 8 (over y, x, core).
Axes of the slice: x: 2, y: 2, z: 4, core: 2. Of those that a mesh axis runs over, the one named last changes fastest.
Arguments:
- source_spectra: bfloat16 [2, 384, 16384], P(None, 'rcv', 'src'), may hold values from -6 to 6
- receiver_spectra: bfloat16 [2, 384, 16384], P(None, 'src', 'rcv'), may hold values from -6 to 6
- source_phase: float32 [16384, 384], P('src'), may hold values from -3.140625 to 3.140625
- receiver_phase: float32 [16384, 384], P('rcv'), may hold values from -3.140625 to 3.140625
Outputs:
- beam_power: float32 [384, 2, 384], P('src', None, 'rcv')
All inputs are finite; a program needn't handle non-finite values.
Results may differ from a plain program's by a relative error of at most 0.025.
Values may be sent and summed in bfloat16 or wider, within the bound.
No kernel may reach another device: no remote copies, remote signals or barrier semaphores. Data moves between devices by JAX's collectives and lax.ppermute only.
A program may use at most 192 MiB of HBM per device.

v0:
```python
import math

import jax
import jax.numpy as jnp
from jax import lax
from jax.sharding import PartitionSpec as P

CS = 16384
CR = 16384


def pair_matrix(first, second):
    upper = jnp.concatenate([first, second], 1)
    lower = jnp.concatenate([second, -first], 1)
    return jnp.concatenate([upper, lower], 0)


def compress(correlation):
    half = correlation.shape[1] // 2
    squares = correlation[:, :half] ** 2 + correlation[:, half:] ** 2
    factor = lax.rsqrt(1.0 + squares)
    return correlation * jnp.concatenate([factor, factor], 1)


def steering_matrix(angles, width):
    steer_real = (jnp.cos(angles) / math.sqrt(width)).astype(jnp.bfloat16)
    steer_imag = (jnp.sin(angles) / math.sqrt(width)).astype(jnp.bfloat16)
    upper = jnp.concatenate([steer_real, steer_imag], 1)
    lower = jnp.concatenate([-steer_imag, steer_real], 1)
    return jnp.concatenate([upper, lower], 0)


def shards(source_spectra, receiver_spectra, source_phase, receiver_phase):
    whole_receiver = lax.all_gather(receiver_spectra, "src", axis=1, tiled=True)
    windows = whole_receiver.shape[1]
    recv_real = whole_receiver[0]
    recv_imag = whole_receiver[1]
    source_width = source_spectra.shape[2]
    piece = lax.all_gather(source_spectra, "rcv", axis=1, tiled=True)
    length = piece.shape[1]
    right_side = pair_matrix(recv_real, recv_imag)
    left_side = piece.reshape(2 * length, source_width)
    correlation = lax.dot_general(
        left_side, right_side, (((0,), (0,)), ((), ())), preferred_element_type=jnp.float32
    )
    correlation = correlation * (1.0 / math.sqrt(2.0 * windows))
    tile = compress(correlation).astype(jnp.bfloat16)
    steering = steering_matrix(receiver_phase, CR)
    partial_beams = jnp.dot(tile, steering, preferred_element_type=jnp.float32).astype(jnp.bfloat16)
    beam_width = receiver_phase.shape[1]
    src_real = (jnp.cos(source_phase) / math.sqrt(CS)).astype(jnp.bfloat16)
    src_imag = (jnp.sin(source_phase) / math.sqrt(CS)).astype(jnp.bfloat16)
    left_side = jnp.concatenate([src_real, src_imag], 0)
    right_side = pair_matrix(partial_beams[:, :beam_width], partial_beams[:, beam_width:])
    beams = lax.dot_general(
        left_side, right_side, (((0,), (0,)), ((), ())), preferred_element_type=jnp.float32
    )
    beams = beams.reshape(beams.shape[0], 2, beam_width)
    narrow = lax.psum_scatter(beams.astype(jnp.bfloat16), "rcv", scatter_dimension=2, tiled=True)
    return lax.psum_scatter(narrow, "src", scatter_dimension=0, tiled=True).astype(jnp.float32)


def solution(mesh):
    placed = (P(None, "rcv", "src"), P(None, "src", "rcv"), P("src", None), P("rcv", None))
    return jax.shard_map(
        shards, mesh=mesh, in_specs=placed, out_specs=P("src", None, "rcv"), check_vma=False
    )
```

profile of v0, /device:TPU:0, one launch (start us, length us, event | category | flops | bytes accessed | tf_op | source)
XLA Modules:
  0.0 325.7 jit_solution(12047032695941313626)
XLA Ops:
  6.5 0.7 all-gather.3.cloned.1.call-update
  7.3 0.0 all-gather.5.cloned.1.call-start
  7.3 0.7 all-gather.5.cloned.1.call-update
  8.0 0.0 reduce-scatter.5.cloned.1.call-start
  8.1 12.1 %multiply_convert_fusion.3 = bf16[2048,384]{1,0:T(8,128)(2,1)} fusion(f32[2048,384]{1,0:T(8,128)} %param.7), kind=kLoop, calls=%fused_computation.37 | loop fusion | flops 1572864 | bytes 4718592 | tf_op jit(solution)/shard_map/convert_element_type | solution.py:26
  20.1 11.3 %fusion.42 = (bf16[2048,384]{1,0:T(8,128)(2,1)}, bf16[2048,384]{1,0:T(8,128)(2,1)}) fusion(f32[2048,384]{1,0:T(8,128)S(1)} %copy-done), kind=kLoop, calls=%fused_computation.46 | loop fusion | flops 3932160 | bytes 6291456 | tf_op jit(solution)/shard_map/neg | solution.py:29
  31.4 23.5 %multiply_convert_fusion.1 = (bf16[4096,384]{1,0:T(8,128)(2,1)S(1)}, bf16[4096,384]{1,0:T(8,128)(2,1)}) fusion(f32[4096,384]{1,0:T(8,128)S(1)} %copy-done.1), kind=kLoop, calls=%fused_computation.34 | loop fusion | flops 6291456 | bytes 12582912 | tf_op jit(solution)/shard_map/convert_element_type | solution.py:51
  54.9 20.2 %all-gather.3.cloned.1.call-done = bf16[2,384,2048]{2,1,0:T(8,128)(2,1)} async-done(((bf16[2,96,2048]{2,1,0:T(8,128)(2,1)}), bf16[2,384,2048]{2,1,0:T(8,128)(2,1)}) %all-gather.3.cloned.1.call-update) | async-done | bytes 3145744 | tf_op jit(solution)/shard_map/all_gather | solution.py:34
  75.1 2.6 fusion.41
  77.8 4.1 %slice_bitcast_fusion.1 = (bf16[384,2048]{1,0:T(8,128)(2,1)}, bf16[384,2048]{1,0:T(8,128)(2,1)}) fusion(bf16[2,384,2048]{2,1,0:T(8,128)(2,1)} %all-gather.3.cloned.1.call-done), kind=kLoop, calls=%fused_computation.39 | loop fusion | bytes 6291456 | tf_op jit(solution)/shard_map/squeeze | solution.py:36
  81.9 39.4 %all-gather.5.cloned.1.call-done = bf16[2,384,4096]{2,1,0:T(8,128)(2,1)} async-done(((bf16[2,48,4096]{2,1,0:T(8,128)(2,1)}), bf16[2,384,4096]{2,1,0:T(8,128)(2,1)}) %all-gather.5.cloned.1.call-update) | async-done | bytes 6291472 | tf_op jit(solution)/shard_map/all_gather | solution.py:39
  121.3 36.8 %multiply_bitcast_fusion = f32[4096,4096]{0,1:T(8,128)} fusion(bf16[768,4096]{1,0:T(8,128)(2,1)} %bitcast.17, bf16[384,2048]{1,0:T(8,128)(2,1)} %fusion.41, bf16[384,2048]{1,0:T(8,128)(2,1)} %get-tuple-element.12, bf16[384,2048]{1,0:T(8,128)(2,1)} %get-tuple-element.11), kind=kOutput, calls=%fused_computation.2 | convolution fusion | flops 25811746816 | bytes 78118912 | tf_op jit(solution)/shard_map/dot_general | solution.py:43
  158.1 33.2 %fusion.3 = f32[4096,2048]{0,1:T(8,128)} fusion(f32[4096,4096]{0,1:T(8,128)} %multiply_bitcast_fusion), kind=kLoop, calls=%fused_computation.6 | loop fusion | flops 33554432 | bytes 100663296 | tf_op jit(solution)/shard_map/rsqrt | solution.py:21
  191.4 51.5 %fusion.12 = bf16[4096,768]{1,0:T(8,128)(2,1)} fusion(f32[4096,4096]{0,1:T(8,128)} %multiply_bitcast_fusion, f32[4096,2048]{0,1:T(8,128)} %fusion.3, bf16[2048,384]{1,0:T(8,128)(2,1)} %multiply_convert_fusion.3, bf16[2048,384]{1,0:T(8,128)(2,1)} %get-tuple-element.5, bf16[2048,384]{1,0:T(8,128)(2,1)} %get-tuple-element.6), kind=kOutput, calls=%fused_computation.15 | convolution fusion | flops 25848446976 | bytes 111673344 | tf_op jit(solution)/shard_map/dot_general | solution.py:49
  242.9 6.0 %fusion.43 = (bf16[4096,384]{1,0:T(8,128)(2,1)}, bf16[4096,384]{1,0:T(8,128)(2,1)}) fusion(bf16[4096,768]{1,0:T(8,128)(2,1)} %fusion.12), kind=kLoop, calls=%fused_computation.47 | loop fusion | flops 1572864 | bytes 12582912 | tf_op jit(solution)/shard_map/slice | solution.py:54
  248.9 11.5 %fusion.32 = bf16[384,768]{1,0:T(8,128)(2,1)} fusion(bf16[4096,384]{1,0:T(8,128)(2,1)} %get-tuple-element.10, bf16[4096,384]{1,0:T(8,128)(2,1)} %get-tuple-element.9, bf16[4096,768]{1,0:T(8,128)(2,1)} %fusion.12, bf16[4096,384]{1,0:T(8,128)(2,1)} %get-tuple-element.8, bf16[4096,384]{1,0:T(8,128)(2,1)S(1)} %get-tuple-element.7), kind=kOutput, calls=%fused_computation.40 | convolution fusion | flops 4882464768 | bytes 19464192 | tf_op jit(solution)/shard_map/dot_general | solution.py:55
  260.4 2.1 copy.7
  262.5 0.0 reduce-scatter.5.cloned.1.call-update
  262.5 0.0 reduce-scatter.7.cloned.1.call-start
  262.6 33.9 %reduce-scatter.5.cloned.1.call-done = bf16[384,2,48]{0,2,1:T(8,128)(2,1)} async-done(((bf16[384,2,384]{0,2,1:T(8,128)(2,1)}), bf16[384,2,48]{0,2,1:T(8,128)(2,1)}) %reduce-scatter.5.cloned.1.call-update) | async-done | bytes 73744 | tf_op jit(solution)/shard_map/reduce_scatter | solution.py:59
  296.5 1.6 copy.10
  298.1 19.6 %reduce-scatter.7.cloned.1.call-done = bf16[96,96]{1,0:T(8,128)(2,1)} async-done(((bf16[384,96]{1,0:T(8,128)(2,1)}), bf16[96,96]{1,0:T(8,128)(2,1)}) %reduce-scatter.7.cloned.1.call-update) | async-done | bytes 18448
  317.7 0.8 copy.11
  318.6 0.6 convert_element_type.35
  (6 shorter events, 0.0 us)
Async XLA Ops:
  6.5 13.6 %copy-start = (f32[2048,384]{1,0:T(8,128)S(1)}, f32[2048,384]{1,0:T(8,128)}, u32[]{:S(2)}) copy-start(f32[2048,384]{1,0:T(8,128)} %param.7) | copy-start | bytes 9437188
  6.5 68.6 %all-gather.3.cloned.1.call-start = ((), (), s32[]{:S(2)}) async-start(), calls=%async_computation.2 | async-start | bytes 3932160 | tf_op jit(solution)/shard_map/all_gather | solution.py:34
  7.3 114.0 %all-gather.5.cloned.1.call-start = ((), (), s32[]{:S(2)}) async-start(), calls=%async_computation.3 | async-start | bytes 7077888 | tf_op jit(solution)/shard_map/all_gather | solution.py:39
  8.0 288.5 %reduce-scatter.5.cloned.1.call-start = ((), (), s32[]{:S(2)}) async-start(), calls=%async_computation.4 | async-start | bytes 663552 | tf_op jit(solution)/shard_map/reduce_scatter | solution.py:59
  8.1 23.4 %copy-start.1 = (f32[4096,384]{1,0:T(8,128)S(1)}, f32[4096,384]{1,0:T(8,128)}, u32[]{:S(2)}) copy-start(f32[4096,384]{1,0:T(8,128)} %param.6) | copy-start | bytes 18874372
  262.5 55.2 %reduce-scatter.7.cloned.1.call-start = ((), (), s32[]{:S(2)}) async-start(), calls=%async_computation.5 | async-start | bytes 122880
Sparse Core Ops, SparseCore 0:
  8.9 66.1 all-gather.2
  77.0 44.2 all-gather.4
  262.6 33.8 reduce-scatter.4
  298.6 19.0 reduce-scatter.6
where the time goes:
time: 326 us
  waiting for transfers between devices  115 us (35%)
  matrix products  99.8 us (31%)
  other arithmetic  89.4 us (27%)
  between operations  13.1 us (4%)
  local copies, waits for them, and re-layouts  8.68 us (3%)
    dot_general x1, matrix products, shards(): jnp.dot(tile, steering, preferred_element_type=jnp.float32)  51.5 us
    dot_general x2, matrix products, shards(): lax.dot_general(left_side, right_side, (((0,), (0,)), ((), ())), preferre...  48.3 us
    all_gather x1, waiting for transfers between devices, shards(): piece = lax.all_gather(source_spectra, 'rcv', axis=1, tiled=True)  39.4 us
    reduce_scatter x1, waiting for transfers between devices, shards(): lax.psum_scatter(beams.astype(jnp.bfloat16), 'rcv', scatter_dimension=2,...  33.9 us
    rsqrt x1, other arithmetic, compress(): factor = lax.rsqrt(1.0 + squares)  33.2 us
    convert_element_type x1, other arithmetic, shards(): src_real = (jnp.cos(source_phase) / math.sqrt(CS)).astype(jnp.bfloat16)  23.5 us
    unnamed x5, waiting for transfers between devices  21 us
    all_gather x1, waiting for transfers between devices, shards(): whole_receiver = lax.all_gather(receiver_spectra, 'src', axis=1, tiled=True)  20.2 us
  transfers between devices with their start and end apart: 4, of which 4 were waited for; matrix products, arithmetic and copies ran while one was open for 16% of the time, Pallas kernels for 0%

commit v1 on v0

v1 whole, which is shorter than its diff:
```python
import functools
import math

import jax
import jax.numpy as jnp
from jax import lax
from jax.experimental import pallas as pl
from jax.experimental.pallas import tpu as pltpu
from jax.sharding import PartitionSpec as P

F32 = jnp.float32
BF16 = jnp.bfloat16
VMEM_LIMIT = 60 << 20
HBM = pl.BlockSpec(memory_space=pltpu.HBM)


def sin_cos(angle, scale):
    half = angle * 0.5
    y = half * half
    s = 2.59040812e-6
    for coef in (-1.98008581e-4, 8.33289918e-3, -1.66666476e-1, 9.99999977e-1):
        s = s * y + coef
    s = s * half
    c = 2.31531323e-5
    for coef in (-1.38536698e-3, 4.16635801e-2, -4.99999052e-1, 9.99999953e-1):
        c = c * y + coef
    s2 = s * (2.0 * scale)
    return s2 * c, scale - s2 * s


def source_steer_kernel(scale, phase_ref, out_ref):
    sin, cos = sin_cos(phase_ref[...].T, scale)
    out_ref[0] = cos.astype(BF16)
    out_ref[1] = (cos + sin).astype(BF16)
    out_ref[2] = (cos - sin).astype(BF16)


def receiver_steer_kernel(scale, phase_ref, out_ref):
    width = phase_ref.shape[1]
    sin, cos = sin_cos(phase_ref[...], scale)
    out_ref[:, :width] = cos.astype(BF16)
    out_ref[:, width:] = sin.astype(BF16)


def steering(kernel, phase, total, steps, shape, block, where):
    return pl.pallas_call(
        functools.partial(kernel, 1.0 / math.sqrt(total)),
        grid=(steps,),
        in_specs=[pl.BlockSpec((phase.shape[0] // steps, phase.shape[1]), lambda i: (i, 0))],
        out_specs=pl.BlockSpec(block, where),
        out_shape=jax.ShapeDtypeStruct(shape, BF16),
        compiler_params=pltpu.CompilerParams(vmem_limit_bytes=VMEM_LIMIT),
        cost_estimate=pl.CostEstimate(
            flops=phase.size // 100, bytes_accessed=phase.size // 100, transcendentals=0
        ),
    )(phase)


def nt(x, y):
    return lax.dot_general(x, y, (((1,), (1,)), ((), ())), preferred_element_type=F32)


def nn(x, y):
    return jnp.dot(x, y, preferred_element_type=F32)


def split(windows):
    three = windows // 256 * 256
    return three, windows - three


def place(j, ct, windows, pieces, where, right):
    wg, ws = split(windows)
    depth = wg + 2 * ws

    def fill(ref, w0):
        height = ref.shape[1]
        cut = min(max(wg - w0, 0), height)
        if cut:
            p = ref[0, :cut, :]
            q = ref[1, :cut, :]
            right[w0 : w0 + cut, :] = q
            right[depth + w0 : depth + w0 + cut, :] = p
            right[2 * depth + w0 : 2 * depth + w0 + cut, :] = p - q
        if cut < height:
            rows = height - cut
            for base in (w0 + cut, depth + w0 + cut):
                right[base : base + rows, :] = ref[0, cut:, :]
                right[base + ws : base + ws + rows, :] = ref[1, cut:, :]

    for ref, (w0, low, high, whole) in zip(pieces, where):
        if whole:
            fill(ref, w0)
        else:
            pl.when(jnp.logical_and(j >= low // ct, j < high // ct))(functools.partial(fill, ref, w0))


def beam_kernel(plan, *refs):
    windows, rc, r_start, rows, ct, s_where, r_parts, first, fold = plan
    table = refs[0]
    n_r = len(r_parts)
    r_refs = refs[1 : 1 + n_r]
    s_refs = refs[1 + n_r : 1 + n_r + len(s_where)]
    rest = refs[1 + n_r + len(s_where) :]
    csteer, rsteer = rest[:2]
    before = None if first else rest[2]
    outs = rest[2 if first else 3 : -7]
    right, rbuf, left_re, left_im, left_x, acc, r_sem = rest[-7:]
    wg, ws = split(windows)
    depth = wg + 2 * ws
    step = pl.program_id(0)

    @pl.when(step == 0)
    def _():
        r_copies = []
        for ref, parts in zip(r_refs, r_parts):
            piece = ref.shape[1] // parts
            for part in range(parts):
                row = len(r_copies)
                dest = pl.multiple_of(table[1 + row], 16)
                copy = pltpu.make_async_copy(
                    ref.at[:, pl.ds(part * piece, piece), :], rbuf.at[:, pl.ds(dest, piece), :], r_sem.at[row]
                )
                copy.start()
                r_copies.append(copy)
        acc[...] = jnp.zeros_like(acc)
        for copy in r_copies:
            copy.wait()

        @pl.loop(0, rc // rows)
        def _(block):
            where = pl.ds(pl.multiple_of(block * rows, rows), rows)
            x = rbuf[0, :, where]
            y = rbuf[1, :, where]
            left_re[where, :wg] = (x[:wg] + y[:wg]).T
            left_im[where, :wg] = (y[:wg] - x[:wg]).T
            left_x[where, :] = x[:wg].T
            if ws:
                xt = x[wg:].T
                yt = y[wg:].T
                left_re[where, wg : wg + ws] = xt
                left_re[where, wg + ws :] = yt
                left_im[where, wg : wg + ws] = yt
                left_im[where, wg + ws :] = -xt

    place(step, ct, windows, s_refs, s_where, right)

    @pl.loop(0, rc // rows)
    def _(block):
        where = pl.ds(pl.multiple_of(block * rows, rows), rows)
        common = nn(left_x[where, :], right[2 * depth :, :])
        real = nn(left_re[where, :], right[:depth, :]) + common
        imag = nn(left_im[where, :], right[depth : 2 * depth, :]) + common
        factor = lax.rsqrt(2.0 * windows + real * real + imag * imag)
        real = real * factor
        imag = imag * factor
        both = nt(csteer[0], (real + imag).astype(BF16))
        first_part = nt(csteer[1], real.astype(BF16))
        second_part = nt(csteer[2], imag.astype(BF16))
        acc[0, :, where] += both - second_part
        acc[1, :, where] += both - first_part

    @pl.when(step == pl.num_programs(0) - 1)
    def _():
        steer = rsteer[r_start : r_start + rc, :]
        width = steer.shape[1] // 2
        upper = nn(acc[0].astype(BF16), steer)
        lower = nn(acc[1].astype(BF16), steer)
        real = upper[:, :width] - lower[:, width:]
        imag = upper[:, width:] + lower[:, :width]
        if not first:
            real = real + before[:, :width]
            imag = imag + before[:, width:]
        if fold is None:
            outs[0][:, :width] = real
            outs[0][:, width:] = imag
        else:
            groups, paired = fold
            piece = width // groups
            real = real.T.astype(BF16)
            imag = imag.T.astype(BF16)
            for k in range(groups):
                both = jnp.concatenate(
                    [real[k * piece : (k + 1) * piece, :], imag[k * piece : (k + 1) * piece, :]], 0
                )
                if not paired:
                    outs[0][k] = both
                else:
                    slot = jnp.bitwise_xor(table[0], k)

                    @pl.when(slot % 2 == 0)
                    def _():
                        outs[0][slot // 2] = both

                    @pl.when(slot % 2 == 1)
                    def _():
                        outs[1][slot // 2] = both


def beam_call(table, r_pieces, r_parts, s_pieces, s_where, csteer, rsteer, before, r_start, windows, fold):
    n_a, total_c = csteer.shape[1:]
    n_b = rsteer.shape[1] // 2
    rc = r_pieces[0].shape[-1]
    rows = min(512, rc)
    ct = min([1024] + [high - low for _, low, high in s_where])
    wg, ws = split(windows)
    depth = wg + 2 * ws
    first = before is None
    s_where = tuple((*spot, spot[2] - spot[1] == total_c) for spot in s_where)
    if fold is None:
        out_shape = [jax.ShapeDtypeStruct((n_a, 2 * n_b), F32)]
    else:
        groups, paired = fold
        half = groups // 2 if paired else groups
        out_shape = [jax.ShapeDtypeStruct((half, 2 * n_b // groups, n_a), BF16)] * (2 if paired else 1)
    args = [table] + list(r_pieces) + list(s_pieces) + [csteer, rsteer]
    specs = [pl.BlockSpec(memory_space=pltpu.SMEM)] + [HBM] * len(r_pieces)
    for piece, (_, low, high, _) in zip(s_pieces, s_where):
        specs.append(
            pl.BlockSpec(
                (2, piece.shape[1], ct),
                lambda j, low=low, high=high: (0, 0, jnp.clip(j - low // ct, 0, (high - low) // ct - 1)),
            )
        )
    specs += [
        pl.BlockSpec((3, n_a, ct), lambda j: (0, 0, j)),
        pl.BlockSpec(rsteer.shape, lambda j: (0, 0)),
    ]
    if not first:
        args.append(before)
        specs.append(pl.BlockSpec(before.shape, lambda j: (0, 0)))
    plan = (windows, rc, r_start, rows, ct, s_where, r_parts, first, fold)
    return pl.pallas_call(
        functools.partial(beam_kernel, plan),
        grid=(total_c // ct,),
        out_shape=out_shape,
        in_specs=specs,
        out_specs=[pl.BlockSpec(shape.shape, lambda j, n=len(shape.shape): (0,) * n) for shape in out_shape],
        scratch_shapes=[
            pltpu.VMEM((2 * depth + wg, ct), BF16),
            pltpu.VMEM((2, windows, rc), BF16),
            pltpu.VMEM((rc, depth), BF16),
            pltpu.VMEM((rc, depth), BF16),
            pltpu.VMEM((rc, wg), BF16),
            pltpu.VMEM((2, n_a, rc), F32),
            pltpu.SemaphoreType.DMA((sum(r_parts),)),
        ],
        compiler_params=pltpu.CompilerParams(vmem_limit_bytes=VMEM_LIMIT),
        cost_estimate=pl.CostEstimate(
            flops=2 * rc * total_c * (5 * 256 + 3 * n_a), bytes_accessed=16 << 20, transcendentals=0
        ),
    )(*args)


def swap(x, axis, size, mask):
    return lax.ppermute(x, axis, [(i, i ^ mask) for i in range(size)])


def shards(n_src, n_rcv, source_spectra, receiver_spectra, source_phase, receiver_phase):
    height = source_spectra.shape[1]
    deep = receiver_spectra.shape[1]
    windows = n_rcv * height
    c = source_spectra.shape[2]
    r = receiver_spectra.shape[2]
    fast = n_src == 4 and n_rcv == 8 and height % 16 == 0 and deep == 2 * height
    n_a = source_phase.shape[1]
    n_b = receiver_phase.shape[1]
    steps = 8
    c_steering = functools.partial(
        steering, source_steer_kernel, source_phase, c * n_src, steps, (3, n_a, c),
        (3, n_a, c // steps), lambda i: (0, 0, i),
    )
    r_steering = functools.partial(
        steering, receiver_steer_kernel, receiver_phase, r * n_rcv, steps, (r, 2 * n_b),
        (r // steps, 2 * n_b), lambda i: (i, 0),
    )
    barrier = lax.optimization_barrier
    if not fast:
        csteer = c_steering()
        rsteer = r_steering()
        spectra = lax.all_gather(source_spectra, "rcv", axis=1, tiled=True)
        whole = lax.all_gather(receiver_spectra, "src", axis=1, tiled=True)
        (beams,) = beam_call(
            jnp.zeros((2,), jnp.int32), (whole,), (1,), (spectra,), ((0, 0, c),), csteer, rsteer,
            None, 0, windows, (n_rcv, False),
        )
        mine = lax.all_to_all(beams, "rcv", 0, 0).astype(F32).sum(0)
        mine = mine.astype(BF16).T.reshape(n_src, n_a // n_src, mine.shape[0])
        total = lax.all_to_all(mine, "src", 0, 0).astype(F32).sum(0)
        return total.reshape(total.shape[0], 2, total.shape[1] // 2)

    me = lax.axis_index("rcv")
    z = lax.axis_index("src")
    places = [((2 * (z ^ mask) + h) ^ me) * height for mask in range(n_src) for h in (0, 1)]
    table = jnp.stack([me] + places).astype(jnp.int32)
    r_parts = (2,) * n_src
    across, along, diagonal = [swap(source_spectra, "rcv", n_rcv, mask) for mask in (2, 4, 6)]
    own = receiver_spectra[:, :, : r // 2]
    own_b = receiver_spectra[:, :, r // 2 :]
    r_first = [own] + [swap(own, "src", n_src, mask) for mask in range(1, n_src)]
    csteer = c_steering()
    rsteer = r_steering()
    s_pieces, r_first, csteer, rsteer, own_b = barrier(
        ([source_spectra, across, along, diagonal], r_first, csteer, rsteer, own_b)
    )
    s_pieces += [swap(piece, "rcv", n_rcv, 1) for piece in s_pieces]
    s_where = tuple((mask * height, 0, c) for mask in (0, 2, 4, 6, 1, 3, 5, 7))
    r_last = [own_b] + [swap(own_b, "src", n_src, mask) for mask in range(1, n_src)]
    (beams,) = beam_call(table, r_first, r_parts, s_pieces, s_where, csteer, rsteer, None, 0, windows, None)
    keep, send = beam_call(
        table, r_last, r_parts, s_pieces, s_where, csteer, rsteer, beams, r // 2, windows, (n_rcv, True)
    )
    got = swap(send, "rcv", n_rcv, 1)
    part = [keep[j].astype(F32) + got[j].astype(F32) for j in range(n_rcv // 2)]
    moved = [swap(part[j].astype(BF16), "rcv", n_rcv, 2 * j) for j in range(1, n_rcv // 2)]
    mine = part[0]
    for piece in moved:
        mine = mine + piece.astype(F32)
    mine = mine.T.reshape(n_src, n_a // n_src, mine.shape[0])
    total = lax.dynamic_index_in_dim(mine, z, 0, keepdims=False)
    for mask in range(1, n_src):
        piece = lax.dynamic_index_in_dim(mine, z ^ mask, 0, keepdims=False)
        total = total + swap(piece.astype(BF16), "src", n_src, mask).astype(F32)
    return total.reshape(total.shape[0], 2, total.shape[1] // 2)


def solution(mesh):
    n_src, n_rcv = mesh.shape["src"], mesh.shape["rcv"]
    placed = (P(None, "rcv", "src"), P(None, "src", "rcv"), P("src", None), P("rcv", None))
    return jax.shard_map(
        functools.partial(shards, n_src, n_rcv),
        mesh=mesh,
        in_specs=placed,
        out_specs=P("src", None, "rcv"),
        check_vma=False,
    )
```

time: 326 us -> 141 us (0.43)
  matrix products: 99.8 us -> 0 us
  waiting for transfers between devices: 115 us -> 20.9 us
  other arithmetic: 89.4 us -> 1.96 us
  Pallas kernels: 0 us -> 85.6 us
  starting transfers between devices: 0.12 us -> 27.1 us
  between operations: 13.1 us -> 0.21 us
  local copies, waits for them, and re-layouts: 8.68 us -> 4.86 us
    dot_general x3 -> x0, matrix products: 99.8 us -> none  [the longest x1 51.5 us: shards(): jnp.dot(tile, steering, preferred_element_type=jnp.float32)]
    pallas_call x0 -> x4, Pallas kernels: none -> 85.6 us  [the longest x2 67.3 us: beam_call(): pl.pallas_call(functools.partial(beam_kernel, plan), grid=(total_c // ct,...]
    all_gather x2 -> x0, waiting for transfers between devices: 59.6 us -> none  [the longest x1 39.4 us: shards(): piece = lax.all_gather(source_spectra, 'rcv', axis=1, tiled=True)]
    convert_element_type x3 -> x1, other arithmetic: 36.2 us -> 1.01 us  [shards(): part[j].astype(BF16)]
    reduce_scatter x1 -> x0, waiting for transfers between devices: 33.9 us -> none  [shards(): lax.psum_scatter(beams.astype(jnp.bfloat16), 'rcv', scatter_dimension=2,...]
    rsqrt x1 -> x0, other arithmetic: 33.2 us -> none  [compress(): factor = lax.rsqrt(1.0 + squares)]
    ppermute x0 -> x20, starting transfers between devices: none -> 27.1 us  [swap(): return lax.ppermute(x, axis, [(i, i ^ mask) for i in range(size)])]
    unnamed x5 -> x0, waiting for transfers between devices: 21 us -> none
  transfers between devices with their start and end apart: 4 -> 20, of which waited for: 4 -> 8; matrix products, arithmetic and copies ran while one was open for 16% -> 1% of each run, Pallas kernels for 0% -> 37%
where the time goes in v1:
time: 141 us
  Pallas kernels  85.6 us (61%)
  starting transfers between devices  27.1 us (19%)
  waiting for transfers between devices  20.9 us (15%)
  local copies, waits for them, and re-layouts  4.86 us (3%)
  other arithmetic  1.96 us (1%)
    pallas_call x2, Pallas kernels, beam_call(): pl.pallas_call(functools.partial(beam_kernel, plan), grid=(total_c // ct,...  67.3 us
    ppermute x20, starting transfers between devices, swap(): return lax.ppermute(x, axis, [(i, i ^ mask) for i in range(size)])  27.1 us
    ppermute x20, waiting for transfers between devices, swap(): return lax.ppermute(x, axis, [(i, i ^ mask) for i in range(size)])  20.9 us
    pallas_call x2, Pallas kernels, steering(): pl.pallas_call(functools.partial(kernel, 1.0 / math.sqrt(total)), grid=(s...  18.3 us
  transfers between devices with their start and end apart: 20, of which 8 were waited for; matrix products, arithmetic and copies ran while one was open for 1% of the time, Pallas kernels for 37%

profile of v1, /device:TPU:0, one launch (start us, length us, event | category | flops | bytes accessed | tf_op | source)
XLA Modules:
  0.0 140.6 jit_solution(18397659001406261189)
XLA Ops:
  1.2 3.1 %collective-permute-start.3 = (bf16[2,96,1024]{2,1,0:T(8,128)(2,1)S(1)}, bf16[2,96,1024]{2,1,0:T(8,128)(2,1)S(1)}, u32[]{:S(2)}, u32[]{:S(2)}) collective-permute-start(bf16[2,96,1024]{2,1,0:T(8,128)(2,1)S(1)} %get-tuple-element.25.refs_1_), channel_id=1, source_target_pairs={{0,8},{8,0},{16,24},{24,16},{1,9},{9,1},{17,25},{25,17},{2,10},{10... | collective-permute-start | bytes 1179656 | tf_op jit(solution)/shard_map/ppermute | solution.py:256
  4.3 1.5 %collective-permute-start = (bf16[2,48,4096]{2,1,0:T(8,128)(2,1)}, bf16[2,48,4096]{2,1,0:T(8,128)(2,1)S(1)}, u32[]{:S(2)}, u32[]{:S(2)}) collective-permute-start(bf16[2,48,4096]{2,1,0:T(8,128)(2,1)} %refs_5_.1), channel_id=1, source_target_pairs={{0,2},{1,3},{2,0},{3,1},{4,6},{5,7},{6,4},{7,5},{8,10},{9,11},{10,... | collective-permute-start | bytes 2359304 | tf_op jit(solution)/shard_map/ppermute | solution.py:256
  5.8 1.5 %collective-permute-start.1 = (bf16[2,48,4096]{2,1,0:T(8,128)(2,1)}, bf16[2,48,4096]{2,1,0:T(8,128)(2,1)S(1)}, u32[]{:S(2)}, u32[]{:S(2)}) collective-permute-start(bf16[2,48,4096]{2,1,0:T(8,128)(2,1)} %refs_5_.1), channel_id=1, source_target_pairs={{0,4},{1,5},{2,6},{3,7},{4,0},{5,1},{6,2},{7,3},{8,12},{9,13},{10,... | collective-permute-start | bytes 2359304 | tf_op jit(solution)/shard_map/ppermute | solution.py:256
  7.8 2.6 %collective-permute-start.4 = (bf16[2,96,1024]{2,1,0:T(8,128)(2,1)S(1)}, bf16[2,96,1024]{2,1,0:T(8,128)(2,1)S(1)}, u32[]{:S(2)}, u32[]{:S(2)}) collective-permute-start(bf16[2,96,1024]{2,1,0:T(8,128)(2,1)S(1)} %get-tuple-element.25.refs_1_), channel_id=1, source_target_pairs={{0,16},{8,24},{16,0},{24,8},{1,17},{9,25},{17,1},{25,9},{2,18},{10... | collective-permute-start | bytes 1179656 | tf_op jit(solution)/shard_map/ppermute | solution.py:256
  10.4 8.7 %collective-permute-done.3.refs_2_ = bf16[2,96,1024]{2,1,0:T(8,128)(2,1)S(1)} collective-permute-done((bf16[2,96,1024]{2,1,0:T(8,128)(2,1)S(1)}, bf16[2,96,1024]{2,1,0:T(8,128)(2,1)S(1)}, u32[]{:S(2)}, u32[]{:S(2)}) %collective-permute-start.3) | collective-permute-done | bytes 393248 | tf_op jit(solution)/shard_map/ppermute | solution.py:256
  19.1 2.6 %collective-permute-start.5 = (bf16[2,96,1024]{2,1,0:T(8,128)(2,1)S(1)}, bf16[2,96,1024]{2,1,0:T(8,128)(2,1)}, u32[]{:S(2)}, u32[]{:S(2)}) collective-permute-start(bf16[2,96,1024]{2,1,0:T(8,128)(2,1)S(1)} %get-tuple-element.25.refs_1_), channel_id=1, source_target_pairs={{0,24},{8,16},{16,8},{24,0},{1,25},{9,17},{17,9},{25,1},{2,26},{10... | collective-permute-start | bytes 1179656 | tf_op jit(solution)/shard_map/ppermute | solution.py:256
  21.7 7.3 %shard_map.47.refs_14_ = bf16[2048,768]{1,0:T(8,128)(2,1)} custom-call(f32[2048,384]{1,0:T(8,128)} %phase_ref.3), custom_call_target="tpu_custom_call" | custom-call | flops 7864 | bytes 7864 | tf_op jit(solution)/shard_map/pallas_call | solution.py:46
  29.0 11.0 %shard_map.46.refs_13_ = bf16[3,384,4096]{2,1,0:T(8,128)(2,1)} custom-call(f32[4096,384]{1,0:T(8,128)} %phase_ref.2), custom_call_target="tpu_custom_call" | custom-call | flops 15728 | bytes 15728 | tf_op jit(solution)/shard_map/pallas_call | solution.py:46
  40.0 1.5 %collective-permute-done.1.refs_7_ = bf16[2,48,4096]{2,1,0:T(8,128)(2,1)S(1)} collective-permute-done((bf16[2,48,4096]{2,1,0:T(8,128)(2,1)}, bf16[2,48,4096]{2,1,0:T(8,128)(2,1)S(1)}, u32[]{:S(2)}, u32[]{:S(2)}) %collective-permute-start.1) | collective-permute-done | bytes 786464 | tf_op jit(solution)/shard_map/ppermute | solution.py:256
  43.2 2.9 %collective-permute-start.6 = (bf16[2,96,1024]{2,1,0:T(8,128)(2,1)S(1)}, bf16[2,96,1024]{2,1,0:T(8,128)(2,1)S(1)}, u32[]{:S(2)}, u32[]{:S(2)}) collective-permute-start(bf16[2,96,1024]{2,1,0:T(8,128)(2,1)S(1)} %get-tuple-element.18.refs_1_), channel_id=1, source_target_pairs={{0,8},{8,0},{16,24},{24,16},{1,9},{9,1},{17,25},{25,17},{2,10},{10... | collective-permute-start | bytes 1179656 | tf_op jit(solution)/shard_map/ppermute | solution.py:256
  46.1 1.8 %collective-permute-start.7 = (bf16[2,96,1024]{2,1,0:T(8,128)(2,1)S(1)}, bf16[2,96,1024]{2,1,0:T(8,128)(2,1)S(1)}, u32[]{:S(2)}, u32[]{:S(2)}) collective-permute-start(bf16[2,96,1024]{2,1,0:T(8,128)(2,1)S(1)} %get-tuple-element.18.refs_1_), channel_id=1, source_target_pairs={{0,16},{8,24},{16,0},{24,8},{1,17},{9,25},{17,1},{25,9},{2,18},{10... | collective-permute-start | bytes 1179656 | tf_op jit(solution)/shard_map/ppermute | solution.py:256
  47.9 1.4 collective-permute-start.8
  49.3 33.5 %shard_map.48.refs_15_ = f32[384,768]{1,0:T(8,128)} custom-call(s32[9]{0:T(128)} %stack.39.refs_0_, bf16[2,96,1024]{2,1,0:T(8,128)(2,1)} %copy-done.1, bf16[2,96,1024]{2,1,0:T(8,128)(2,1)} %copy-done.5, bf16[2,96,1024]{2,1,0:T(8,128)(2,1)} %copy-done.6, bf16[2,96,1024]{2,1,0:T(8,128)(2,1)} %collective-permute-done.5.refs_4_, bf16[2,48,4096]{2,1,0:T(8,128)(2,1)} %refs_5_.1, ...), custom_call_target="tpu_custom_call" | custom-call | flops 20401094656 | bytes 16777216 | tf_op jit(solution)/shard_map/pallas_call | solution.py:233
  84.5 33.8 %shard_map.49 = (bf16[4,96,384]{2,1,0:T(8,128)(2,1)}, bf16[4,96,384]{2,1,0:T(8,128)(2,1)}) custom-call(s32[9]{0:T(128)} %stack.39.refs_0_, bf16[2,96,1024]{2,1,0:T(8,128)(2,1)} %copy-done, bf16[2,96,1024]{2,1,0:T(8,128)(2,1)} %copy-done.7, bf16[2,96,1024]{2,1,0:T(8,128)(2,1)} %copy-done.8, bf16[2,96,1024]{2,1,0:T(8,128)(2,1)} %copy-done.9, ...), custom_call_target="tpu_custom_call" | custom-call | flops 20401094656 | bytes 16777216 | tf_op jit(solution)/shard_map/pallas_call | solution.py:233
  118.4 1.8 %collective-permute-done.13 = bf16[4,96,384]{2,1,0:T(8,128)(2,1)S(1)} collective-permute-done((bf16[4,96,384]{2,1,0:T(8,128)(2,1)}, bf16[4,96,384]{2,1,0:T(8,128)(2,1)S(1)}, u32[]{:S(2)}, u32[]{:S(2)}) %collective-permute-start.13) | collective-permute-done | bytes 294944 | tf_op jit(solution)/shard_map/ppermute | solution.py:256
  121.2 1.6 %collective-permute-start.14 = (bf16[96,384]{1,0:T(8,128)(2,1)S(1)}, bf16[96,384]{1,0:T(8,128)(2,1)S(1)}, u32[]{:S(2)}, u32[]{:S(2)}) collective-permute-start(bf16[96,384]{1,0:T(8,128)(2,1)S(1)} %get-tuple-element.33), channel_id=1, source_target_pairs={{0,2},{1,3},{2,0},{3,1},{4,6},{5,7},{6,4},{7,5},{8,10},{9,11},{10,... | collective-permute-start | bytes 221192 | tf_op jit(solution)/shard_map/ppermute | solution.py:256
  122.7 1.5 %collective-permute-start.15 = (bf16[96,384]{1,0:T(8,128)(2,1)S(1)}, bf16[96,384]{1,0:T(8,128)(2,1)S(1)}, u32[]{:S(2)}, u32[]{:S(2)}) collective-permute-start(bf16[96,384]{1,0:T(8,128)(2,1)S(1)} %get-tuple-element.35), channel_id=1, source_target_pairs={{0,4},{1,5},{2,6},{3,7},{4,0},{5,1},{6,2},{7,3},{8,12},{9,13},{10,... | collective-permute-start | bytes 221192 | tf_op jit(solution)/shard_map/ppermute | solution.py:256
  125.6 1.5 %collective-permute-done.15 = bf16[96,384]{1,0:T(8,128)(2,1)S(1)} collective-permute-done((bf16[96,384]{1,0:T(8,128)(2,1)S(1)}, bf16[96,384]{1,0:T(8,128)(2,1)S(1)}, u32[]{:S(2)}, u32[]{:S(2)}) %collective-permute-start.15) | collective-permute-done | bytes 73760 | tf_op jit(solution)/shard_map/ppermute | solution.py:256
  127.1 2.4 %collective-permute-done.16 = bf16[96,384]{1,0:T(8,128)(2,1)S(1)} collective-permute-done((bf16[96,384]{1,0:T(8,128)(2,1)S(1)}, bf16[96,384]{1,0:T(8,128)(2,1)S(1)}, u32[]{:S(2)}, u32[]{:S(2)}) %collective-permute-start.16) | collective-permute-done | bytes 73760 | tf_op jit(solution)/shard_map/ppermute | solution.py:256
  130.8 1.5 %collective-permute-start.17 = (bf16[96,96]{1,0:T(8,128)(2,1)S(1)}, bf16[96,96]{1,0:T(8,128)(2,1)S(1)}, u32[]{:S(2)}, u32[]{:S(2)}) collective-permute-start(bf16[96,96]{1,0:T(8,128)(2,1)S(1)} %bitcast.43), channel_id=1, source_target_pairs={{0,8},{8,0},{16,24},{24,16},{1,9},{9,1},{17,25},{25,17},{2,10},{10... | collective-permute-start | bytes 55304 | tf_op jit(solution)/shard_map/ppermute | solution.py:256
  132.5 1.6 %collective-permute-start.18 = (bf16[96,96]{1,0:T(8,128)(2,1)S(1)}, bf16[96,96]{1,0:T(8,128)(2,1)S(1)}, u32[]{:S(2)}, u32[]{:S(2)}) collective-permute-start(bf16[96,96]{1,0:T(8,128)(2,1)S(1)} %bitcast.44), channel_id=1, source_target_pairs={{0,16},{8,24},{16,0},{24,8},{1,17},{9,25},{17,1},{25,9},{2,18},{10... | collective-permute-start | bytes 55304 | tf_op jit(solution)/shard_map/ppermute | solution.py:256
  134.2 1.4 %collective-permute-start.19 = (bf16[96,96]{1,0:T(8,128)(2,1)S(1)}, bf16[96,96]{1,0:T(8,128)(2,1)S(1)}, u32[]{:S(2)}, u32[]{:S(2)}) collective-permute-start(bf16[96,96]{1,0:T(8,128)(2,1)S(1)} %bitcast.45), channel_id=1, source_target_pairs={{0,24},{8,16},{16,8},{24,0},{1,25},{9,17},{17,9},{25,1},{2,26},{10... | collective-permute-start | bytes 55304 | tf_op jit(solution)/shard_map/ppermute | solution.py:256
  135.8 1.7 %collective-permute-done.18 = bf16[96,96]{1,0:T(8,128)(2,1)S(1)} collective-permute-done((bf16[96,96]{1,0:T(8,128)(2,1)S(1)}, bf16[96,96]{1,0:T(8,128)(2,1)S(1)}, u32[]{:S(2)}, u32[]{:S(2)}) %collective-permute-start.18) | collective-permute-done | bytes 18464 | tf_op jit(solution)/shard_map/ppermute | solution.py:256
  137.5 2.4 %collective-permute-done.19 = bf16[96,96]{1,0:T(8,128)(2,1)S(1)} collective-permute-done((bf16[96,96]{1,0:T(8,128)(2,1)S(1)}, bf16[96,96]{1,0:T(8,128)(2,1)S(1)}, u32[]{:S(2)}, u32[]{:S(2)}) %collective-permute-start.19) | collective-permute-done | bytes 18464 | tf_op jit(solution)/shard_map/ppermute | solution.py:256
  (53 shorter events, 9.8 us)
Async XLA Ops:
  1.2 27.8 %copy-start.1 = (bf16[2,96,1024]{2,1,0:T(8,128)(2,1)}, bf16[2,96,1024]{2,1,0:T(8,128)(2,1)S(1)}, u32[]{:S(2)}) copy-start(bf16[2,96,1024]{2,1,0:T(8,128)(2,1)S(1)} %get-tuple-element.25.refs_1_) | copy-start | bytes 1179652
  1.2 46.7 %copy-start = (bf16[2,96,1024]{2,1,0:T(8,128)(2,1)}, bf16[2,96,1024]{2,1,0:T(8,128)(2,1)S(1)}, u32[]{:S(2)}) copy-start(bf16[2,96,1024]{2,1,0:T(8,128)(2,1)S(1)} %get-tuple-element.18.refs_1_) | copy-start | bytes 1179652
  1.2 17.9 %collective-permute-start.3 = (bf16[2,96,1024]{2,1,0:T(8,128)(2,1)S(1)}, bf16[2,96,1024]{2,1,0:T(8,128)(2,1)S(1)}, u32[]{:S(2)}, u32[]{:S(2)}) collective-permute-start(bf16[2,96,1024]{2,1,0:T(8,128)(2,1)S(1)} %get-tuple-element.25.refs_1_), channel_id=1, source_target_pairs={{0,8},{8,0},{16,24},{24,16},{1,9},{9,1},{17,25},{25,17},{2,10},{10... | collective-permute-start | bytes 1179656 | tf_op jit(solution)/shard_map/ppermute | solution.py:256
  4.3 35.7 %collective-permute-start = (bf16[2,48,4096]{2,1,0:T(8,128)(2,1)}, bf16[2,48,4096]{2,1,0:T(8,128)(2,1)S(1)}, u32[]{:S(2)}, u32[]{:S(2)}) collective-permute-start(bf16[2,48,4096]{2,1,0:T(8,128)(2,1)} %refs_5_.1), channel_id=1, source_target_pairs={{0,2},{1,3},{2,0},{3,1},{4,6},{5,7},{6,4},{7,5},{8,10},{9,11},{10,... | collective-permute-start | bytes 2359304 | tf_op jit(solution)/shard_map/ppermute | solution.py:256
  5.8 35.8 %collective-permute-start.1 = (bf16[2,48,4096]{2,1,0:T(8,128)(2,1)}, bf16[2,48,4096]{2,1,0:T(8,128)(2,1)S(1)}, u32[]{:S(2)}, u32[]{:S(2)}) collective-permute-start(bf16[2,48,4096]{2,1,0:T(8,128)(2,1)} %refs_5_.1), channel_id=1, source_target_pairs={{0,4},{1,5},{2,6},{3,7},{4,0},{5,1},{6,2},{7,3},{8,12},{9,13},{10,... | collective-permute-start | bytes 2359304 | tf_op jit(solution)/shard_map/ppermute | solution.py:256
  7.3 34.3 %collective-permute-start.2 = (bf16[2,48,4096]{2,1,0:T(8,128)(2,1)}, bf16[2,48,4096]{2,1,0:T(8,128)(2,1)}, u32[]{:S(2)}, u32[]{:S(2)}) collective-permute-start(bf16[2,48,4096]{2,1,0:T(8,128)(2,1)} %refs_5_.1), channel_id=1, source_target_pairs={{0,6},{1,7},{2,4},{3,5},{4,2},{5,3},{6,0},{7,1},{8,14},{9,15},{10,... | collective-permute-start | bytes 2359304 | tf_op jit(solution)/shard_map/ppermute | solution.py:256
  7.8 32.2 %collective-permute-start.4 = (bf16[2,96,1024]{2,1,0:T(8,128)(2,1)S(1)}, bf16[2,96,1024]{2,1,0:T(8,128)(2,1)S(1)}, u32[]{:S(2)}, u32[]{:S(2)}) collective-permute-start(bf16[2,96,1024]{2,1,0:T(8,128)(2,1)S(1)} %get-tuple-element.25.refs_1_), channel_id=1, source_target_pairs={{0,16},{8,24},{16,0},{24,8},{1,17},{9,25},{17,1},{25,9},{2,18},{10... | collective-permute-start | bytes 1179656 | tf_op jit(solution)/shard_map/ppermute | solution.py:256
  19.1 20.9 %copy-start.5 = (bf16[2,96,1024]{2,1,0:T(8,128)(2,1)}, bf16[2,96,1024]{2,1,0:T(8,128)(2,1)S(1)}, u32[]{:S(2)}) copy-start(bf16[2,96,1024]{2,1,0:T(8,128)(2,1)S(1)} %collective-permute-done.3.refs_2_) | copy-start | bytes 1179652
  19.1 20.9 %collective-permute-start.5 = (bf16[2,96,1024]{2,1,0:T(8,128)(2,1)S(1)}, bf16[2,96,1024]{2,1,0:T(8,128)(2,1)}, u32[]{:S(2)}, u32[]{:S(2)}) collective-permute-start(bf16[2,96,1024]{2,1,0:T(8,128)(2,1)S(1)} %get-tuple-element.25.refs_1_), channel_id=1, source_target_pairs={{0,24},{8,16},{16,8},{24,0},{1,25},{9,17},{17,9},{25,1},{2,26},{10... | collective-permute-start | bytes 1179656 | tf_op jit(solution)/shard_map/ppermute | solution.py:256
  29.0 13.2 %copy-start.2 = (bf16[2,48,4096]{2,1,0:T(8,128)(2,1)S(1)}, bf16[2,48,4096]{2,1,0:T(8,128)(2,1)}, u32[]{:S(2)}) copy-start(bf16[2,48,4096]{2,1,0:T(8,128)(2,1)} %refs_5_.1) | copy-start | bytes 2359300
  41.6 4.6 %collective-permute-start.10 = (bf16[2,48,4096]{2,1,0:T(8,128)(2,1)S(1)}, bf16[2,48,4096]{2,1,0:T(8,128)(2,1)}, u32[]{:S(2)}, u32[]{:S(2)}) collective-permute-start(bf16[2,48,4096]{2,1,0:T(8,128)(2,1)S(1)} %collective-permute-done.refs_6_), channel_id=1, source_target_pairs={{0,1},{1,0},{2,3},{3,2},{4,5},{5,4},{6,7},{7,6},{8,9},{9,8},{10,11... | collective-permute-start | bytes 2359304 | tf_op jit(solution)/shard_map/ppermute | solution.py:256
  41.6 6.4 %collective-permute-start.11 = (bf16[2,48,4096]{2,1,0:T(8,128)(2,1)S(1)}, bf16[2,48,4096]{2,1,0:T(8,128)(2,1)}, u32[]{:S(2)}, u32[]{:S(2)}) collective-permute-start(bf16[2,48,4096]{2,1,0:T(8,128)(2,1)S(1)} %collective-permute-done.1.refs_7_), channel_id=1, source_target_pairs={{0,1},{1,0},{2,3},{3,2},{4,5},{5,4},{6,7},{7,6},{8,9},{9,8},{10,11... | collective-permute-start | bytes 2359304 | tf_op jit(solution)/shard_map/ppermute | solution.py:256
  42.1 7.2 %collective-permute-start.12 = (bf16[2,48,4096]{2,1,0:T(8,128)(2,1)}, bf16[2,48,4096]{2,1,0:T(8,128)(2,1)}, u32[]{:S(2)}, u32[]{:S(2)}) collective-permute-start(bf16[2,48,4096]{2,1,0:T(8,128)(2,1)} %collective-permute-done.2.refs_8_), channel_id=1, source_target_pairs={{0,1},{1,0},{2,3},{3,2},{4,5},{5,4},{6,7},{7,6},{8,9},{9,8},{10,11... | collective-permute-start | bytes 2359304 | tf_op jit(solution)/shard_map/ppermute | solution.py:256
  42.1 7.1 %collective-permute-start.9 = (bf16[2,48,4096]{2,1,0:T(8,128)(2,1)S(1)}, bf16[2,48,4096]{2,1,0:T(8,128)(2,1)}, u32[]{:S(2)}, u32[]{:S(2)}) collective-permute-start(bf16[2,48,4096]{2,1,0:T(8,128)(2,1)S(1)} %copy-done.2), channel_id=1, source_target_pairs={{0,1},{1,0},{2,3},{3,2},{4,5},{5,4},{6,7},{7,6},{8,9},{9,8},{10,11... | collective-permute-start | bytes 2359304 | tf_op jit(solution)/shard_map/ppermute | solution.py:256
  43.2 39.6 %collective-permute-start.6 = (bf16[2,96,1024]{2,1,0:T(8,128)(2,1)S(1)}, bf16[2,96,1024]{2,1,0:T(8,128)(2,1)S(1)}, u32[]{:S(2)}, u32[]{:S(2)}) collective-permute-start(bf16[2,96,1024]{2,1,0:T(8,128)(2,1)S(1)} %get-tuple-element.18.refs_1_), channel_id=1, source_target_pairs={{0,8},{8,0},{16,24},{24,16},{1,9},{9,1},{17,25},{25,17},{2,10},{10... | collective-permute-start | bytes 1179656 | tf_op jit(solution)/shard_map/ppermute | solution.py:256
  46.1 36.7 %collective-permute-start.7 = (bf16[2,96,1024]{2,1,0:T(8,128)(2,1)S(1)}, bf16[2,96,1024]{2,1,0:T(8,128)(2,1)S(1)}, u32[]{:S(2)}, u32[]{:S(2)}) collective-permute-start(bf16[2,96,1024]{2,1,0:T(8,128)(2,1)S(1)} %get-tuple-element.18.refs_1_), channel_id=1, source_target_pairs={{0,16},{8,24},{16,0},{24,8},{1,17},{9,25},{17,1},{25,9},{2,18},{10... | collective-permute-start | bytes 1179656 | tf_op jit(solution)/shard_map/ppermute | solution.py:256
  47.9 34.9 %collective-permute-start.8 = (bf16[2,96,1024]{2,1,0:T(8,128)(2,1)S(1)}, bf16[2,96,1024]{2,1,0:T(8,128)(2,1)S(1)}, u32[]{:S(2)}, u32[]{:S(2)}) collective-permute-start(bf16[2,96,1024]{2,1,0:T(8,128)(2,1)S(1)} %get-tuple-element.18.refs_1_), channel_id=1, source_target_pairs={{0,24},{8,16},{16,8},{24,0},{1,25},{9,17},{17,9},{25,1},{2,26},{10... | collective-permute-start | bytes 1179656 | tf_op jit(solution)/shard_map/ppermute | solution.py:256
  118.3 1.9 %collective-permute-start.13 = (bf16[4,96,384]{2,1,0:T(8,128)(2,1)}, bf16[4,96,384]{2,1,0:T(8,128)(2,1)S(1)}, u32[]{:S(2)}, u32[]{:S(2)}) collective-permute-start(bf16[4,96,384]{2,1,0:T(8,128)(2,1)} %get-tuple-element.30), channel_id=1, source_target_pairs={{0,1},{1,0},{2,3},{3,2},{4,5},{5,4},{6,7},{7,6},{8,9},{9,8},{10,11... | collective-permute-start | bytes 884744 | tf_op jit(solution)/shard_map/ppermute | solution.py:256
  121.2 4.4 %collective-permute-start.14 = (bf16[96,384]{1,0:T(8,128)(2,1)S(1)}, bf16[96,384]{1,0:T(8,128)(2,1)S(1)}, u32[]{:S(2)}, u32[]{:S(2)}) collective-permute-start(bf16[96,384]{1,0:T(8,128)(2,1)S(1)} %get-tuple-element.33), channel_id=1, source_target_pairs={{0,2},{1,3},{2,0},{3,1},{4,6},{5,7},{6,4},{7,5},{8,10},{9,11},{10,... | collective-permute-start | bytes 221192 | tf_op jit(solution)/shard_map/ppermute | solution.py:256
  122.7 4.4 %collective-permute-start.15 = (bf16[96,384]{1,0:T(8,128)(2,1)S(1)}, bf16[96,384]{1,0:T(8,128)(2,1)S(1)}, u32[]{:S(2)}, u32[]{:S(2)}) collective-permute-start(bf16[96,384]{1,0:T(8,128)(2,1)S(1)} %get-tuple-element.35), channel_id=1, source_target_pairs={{0,4},{1,5},{2,6},{3,7},{4,0},{5,1},{6,2},{7,3},{8,12},{9,13},{10,... | collective-permute-start | bytes 221192 | tf_op jit(solution)/shard_map/ppermute | solution.py:256
  124.2 5.3 %collective-permute-start.16 = (bf16[96,384]{1,0:T(8,128)(2,1)S(1)}, bf16[96,384]{1,0:T(8,128)(2,1)S(1)}, u32[]{:S(2)}, u32[]{:S(2)}) collective-permute-start(bf16[96,384]{1,0:T(8,128)(2,1)S(1)} %get-tuple-element.34), channel_id=1, source_target_pairs={{0,6},{1,7},{2,4},{3,5},{4,2},{5,3},{6,0},{7,1},{8,14},{9,15},{10,... | collective-permute-start | bytes 221192 | tf_op jit(solution)/shard_map/ppermute | solution.py:256
  130.8 4.9 %collective-permute-start.17 = (bf16[96,96]{1,0:T(8,128)(2,1)S(1)}, bf16[96,96]{1,0:T(8,128)(2,1)S(1)}, u32[]{:S(2)}, u32[]{:S(2)}) collective-permute-start(bf16[96,96]{1,0:T(8,128)(2,1)S(1)} %bitcast.43), channel_id=1, source_target_pairs={{0,8},{8,0},{16,24},{24,16},{1,9},{9,1},{17,25},{25,17},{2,10},{10... | collective-permute-start | bytes 55304 | tf_op jit(solution)/shard_map/ppermute | solution.py:256
  132.5 5.1 %collective-permute-start.18 = (bf16[96,96]{1,0:T(8,128)(2,1)S(1)}, bf16[96,96]{1,0:T(8,128)(2,1)S(1)}, u32[]{:S(2)}, u32[]{:S(2)}) collective-permute-start(bf16[96,96]{1,0:T(8,128)(2,1)S(1)} %bitcast.44), channel_id=1, source_target_pairs={{0,16},{8,24},{16,0},{24,8},{1,17},{9,25},{17,1},{25,9},{2,18},{10... | collective-permute-start | bytes 55304 | tf_op jit(solution)/shard_map/ppermute | solution.py:256
  134.2 5.7 %collective-permute-start.19 = (bf16[96,96]{1,0:T(8,128)(2,1)S(1)}, bf16[96,96]{1,0:T(8,128)(2,1)S(1)}, u32[]{:S(2)}, u32[]{:S(2)}) collective-permute-start(bf16[96,96]{1,0:T(8,128)(2,1)S(1)} %bitcast.45), channel_id=1, source_target_pairs={{0,24},{8,16},{16,8},{24,0},{1,25},{9,17},{17,9},{25,1},{2,26},{10... | collective-permute-start | bytes 55304 | tf_op jit(solution)/shard_map/ppermute | solution.py:256
  (6 other events, 22.0 us)

commit v2 on v1

--- a/solution.py
+++ b/solution.py
@@ -10,7 +10,7 @@
 
 F32 = jnp.float32
 BF16 = jnp.bfloat16
-VMEM_LIMIT = 60 << 20
+VMEM_LIMIT = (64 << 20) - (512 << 10)
 HBM = pl.BlockSpec(memory_space=pltpu.HBM)
 
 
@@ -69,34 +69,26 @@
     return three, windows - three
 
 
-def place(j, ct, windows, pieces, where, right):
+def place(windows, pieces, where, right):
     wg, ws = split(windows)
     depth = wg + 2 * ws
 
-    def fill(ref, w0):
+    for ref, (w0, planes) in zip(pieces, where):
         height = ref.shape[1]
         cut = min(max(wg - w0, 0), height)
-        if cut:
-            p = ref[0, :cut, :]
-            q = ref[1, :cut, :]
-            right[w0 : w0 + cut, :] = q
-            right[depth + w0 : depth + w0 + cut, :] = p
-            right[2 * depth + w0 : 2 * depth + w0 + cut, :] = p - q
-        if cut < height:
-            rows = height - cut
-            for base in (w0 + cut, depth + w0 + cut):
-                right[base : base + rows, :] = ref[0, cut:, :]
-                right[base + ws : base + ws + rows, :] = ref[1, cut:, :]
-
-    for ref, (w0, low, high, whole) in zip(pieces, where):
-        if whole:
-            fill(ref, w0)
-        else:
-            pl.when(jnp.logical_and(j >= low // ct, j < high // ct))(functools.partial(fill, ref, w0))
+        for number, plane in enumerate(planes):
+            if cut:
+                start = w0 + (0 if plane else depth)
+                right[start : start + cut, :] = ref[number, :cut, :]
+            if cut < height:
+                for base in (0, depth):
+                    start = base + w0 + cut + plane * ws
+                    right[start : start + height - cut, :] = ref[number, cut:, :]
+    right[2 * depth :, :] = right[depth : depth + wg, :] - right[:wg, :]
 
 
 def beam_kernel(plan, *refs):
-    windows, rc, r_start, rows, ct, s_where, r_parts, first, fold = plan
+    windows, rc, r_start, rows, s_where, r_parts, first, fold = plan
     table = refs[0]
     n_r = len(r_parts)
     r_refs = refs[1 : 1 + n_r]
@@ -104,28 +96,24 @@
     rest = refs[1 + n_r + len(s_where) :]
     csteer, rsteer = rest[:2]
     before = None if first else rest[2]
-    outs = rest[2 if first else 3 : -7]
-    right, rbuf, left_re, left_im, left_x, acc, r_sem = rest[-7:]
+    outs = rest[2 if first else 3 : -8]
+    right, rbuf, left_re, left_im, left_x, acc, steer, g_sem = rest[-8:]
     wg, ws = split(windows)
     depth = wg + 2 * ws
     step = pl.program_id(0)
+    g_copy = pltpu.make_async_copy(rsteer.at[pl.ds(r_start, rc), :], steer, g_sem)
 
     @pl.when(step == 0)
     def _():
-        r_copies = []
+        g_copy.start()
+        row = 0
         for ref, parts in zip(r_refs, r_parts):
             piece = ref.shape[1] // parts
             for part in range(parts):
-                row = len(r_copies)
                 dest = pl.multiple_of(table[1 + row], 16)
-                copy = pltpu.make_async_copy(
-                    ref.at[:, pl.ds(part * piece, piece), :], rbuf.at[:, pl.ds(dest, piece), :], r_sem.at[row]
-                )
-                copy.start()
-                r_copies.append(copy)
+                rbuf[:, pl.ds(dest, piece), :] = ref[:, part * piece : (part + 1) * piece, :]
+                row += 1
         acc[...] = jnp.zeros_like(acc)
-        for copy in r_copies:
-            copy.wait()
 
         @pl.loop(0, rc // rows)
         def _(block):
@@ -143,29 +131,29 @@
                 left_im[where, wg : wg + ws] = yt
                 left_im[where, wg + ws :] = -xt
 
-    place(step, ct, windows, s_refs, s_where, right)
+    place(windows, s_refs, s_where, right)
 
     @pl.loop(0, rc // rows)
     def _(block):
         where = pl.ds(pl.multiple_of(block * rows, rows), rows)
         common = nn(left_x[where, :], right[2 * depth :, :])
-        real = nn(left_re[where, :], right[:depth, :]) + common
-        imag = nn(left_im[where, :], right[depth : 2 * depth, :]) + common
-        factor = lax.rsqrt(2.0 * windows + real * real + imag * imag)
+        real = (nn(left_re[where, :], right[:depth, :]) + common).astype(BF16)
+        imag = (nn(left_im[where, :], right[depth : 2 * depth, :]) + common).astype(BF16)
+        factor = lax.rsqrt(real * real + imag * imag + BF16(2 * windows))
         real = real * factor
         imag = imag * factor
-        both = nt(csteer[0], (real + imag).astype(BF16))
-        first_part = nt(csteer[1], real.astype(BF16))
-        second_part = nt(csteer[2], imag.astype(BF16))
+        both = nt(csteer[0], real + imag)
+        first_part = nt(csteer[1], real)
+        second_part = nt(csteer[2], imag)
         acc[0, :, where] += both - second_part
         acc[1, :, where] += both - first_part
 
     @pl.when(step == pl.num_programs(0) - 1)
     def _():
-        steer = rsteer[r_start : r_start + rc, :]
+        g_copy.wait()
         width = steer.shape[1] // 2
-        upper = nn(acc[0].astype(BF16), steer)
-        lower = nn(acc[1].astype(BF16), steer)
+        upper = nn(acc[0].astype(BF16), steer[...])
+        lower = nn(acc[1].astype(BF16), steer[...])
         real = upper[:, :width] - lower[:, width:]
         imag = upper[:, width:] + lower[:, :width]
         if not first:
@@ -201,12 +189,11 @@
     n_a, total_c = csteer.shape[1:]
     n_b = rsteer.shape[1] // 2
     rc = r_pieces[0].shape[-1]
-    rows = min(512, rc)
-    ct = min([1024] + [high - low for _, low, high in s_where])
+    rows = min(1024, rc)
+    ct = min(1024, total_c)
     wg, ws = split(windows)
     depth = wg + 2 * ws
     first = before is None
-    s_where = tuple((*spot, spot[2] - spot[1] == total_c) for spot in s_where)
     if fold is None:
         out_shape = [jax.ShapeDtypeStruct((n_a, 2 * n_b), F32)]
     else:
@@ -214,22 +201,19 @@
         half = groups // 2 if paired else groups
         out_shape = [jax.ShapeDtypeStruct((half, 2 * n_b // groups, n_a), BF16)] * (2 if paired else 1)
     args = [table] + list(r_pieces) + list(s_pieces) + [csteer, rsteer]
-    specs = [pl.BlockSpec(memory_space=pltpu.SMEM)] + [HBM] * len(r_pieces)
-    for piece, (_, low, high, _) in zip(s_pieces, s_where):
-        specs.append(
-            pl.BlockSpec(
-                (2, piece.shape[1], ct),
-                lambda j, low=low, high=high: (0, 0, jnp.clip(j - low // ct, 0, (high - low) // ct - 1)),
-            )
-        )
+    specs = [pl.BlockSpec(memory_space=pltpu.SMEM)] + [
+        pl.BlockSpec(piece.shape, lambda j: (0, 0, 0)) for piece in r_pieces
+    ]
+    for piece in s_pieces:
+        specs.append(pl.BlockSpec((piece.shape[0], piece.shape[1], ct), lambda j: (0, 0, j)))
     specs += [
         pl.BlockSpec((3, n_a, ct), lambda j: (0, 0, j)),
-        pl.BlockSpec(rsteer.shape, lambda j: (0, 0)),
+        HBM,
     ]
     if not first:
         args.append(before)
         specs.append(pl.BlockSpec(before.shape, lambda j: (0, 0)))
-    plan = (windows, rc, r_start, rows, ct, s_where, r_parts, first, fold)
+    plan = (windows, rc, r_start, rows, s_where, r_parts, first, fold)
     return pl.pallas_call(
         functools.partial(beam_kernel, plan),
         grid=(total_c // ct,),
@@ -243,7 +227,8 @@
             pltpu.VMEM((rc, depth), BF16),
             pltpu.VMEM((rc, wg), BF16),
             pltpu.VMEM((2, n_a, rc), F32),
-            pltpu.SemaphoreType.DMA((sum(r_parts),)),
+            pltpu.VMEM((rc, 2 * n_b), BF16),
+            pltpu.SemaphoreType.DMA,
         ],
         compiler_params=pltpu.CompilerParams(vmem_limit_bytes=VMEM_LIMIT),
         cost_estimate=pl.CostEstimate(
@@ -270,18 +255,17 @@
         steering, source_steer_kernel, source_phase, c * n_src, steps, (3, n_a, c),
         (3, n_a, c // steps), lambda i: (0, 0, i),
     )
-    r_steering = functools.partial(
-        steering, receiver_steer_kernel, receiver_phase, r * n_rcv, steps, (r, 2 * n_b),
-        (r // steps, 2 * n_b), lambda i: (i, 0),
+    r_steering = lambda phase: steering(
+        receiver_steer_kernel, phase, r * n_rcv, steps, (r, 2 * n_b), (r // steps, 2 * n_b), lambda i: (i, 0)
     )
     barrier = lax.optimization_barrier
     if not fast:
         csteer = c_steering()
-        rsteer = r_steering()
+        rsteer = r_steering(receiver_phase)
         spectra = lax.all_gather(source_spectra, "rcv", axis=1, tiled=True)
         whole = lax.all_gather(receiver_spectra, "src", axis=1, tiled=True)
         (beams,) = beam_call(
-            jnp.zeros((2,), jnp.int32), (whole,), (1,), (spectra,), ((0, 0, c),), csteer, rsteer,
+            jnp.zeros((2,), jnp.int32), (whole,), (1,), (spectra,), ((0, (0, 1)),), csteer, rsteer,
             None, 0, windows, (n_rcv, False),
         )
         mine = lax.all_to_all(beams, "rcv", 0, 0).astype(F32).sum(0)
@@ -299,12 +283,12 @@
     own_b = receiver_spectra[:, :, r // 2 :]
     r_first = [own] + [swap(own, "src", n_src, mask) for mask in range(1, n_src)]
     csteer = c_steering()
-    rsteer = r_steering()
+    rsteer = r_steering(receiver_phase)
     s_pieces, r_first, csteer, rsteer, own_b = barrier(
         ([source_spectra, across, along, diagonal], r_first, csteer, rsteer, own_b)
     )
     s_pieces += [swap(piece, "rcv", n_rcv, 1) for piece in s_pieces]
-    s_where = tuple((mask * height, 0, c) for mask in (0, 2, 4, 6, 1, 3, 5, 7))
+    s_where = tuple((mask * height, (0, 1)) for mask in (0, 2, 4, 6, 1, 3, 5, 7))
     r_last = [own_b] + [swap(own_b, "src", n_src, mask) for mask in range(1, n_src)]
     (beams,) = beam_call(table, r_first, r_parts, s_pieces, s_where, csteer, rsteer, None, 0, windows, None)
     keep, send = beam_call(

time: 141 us -> 135 us (0.957)
  Pallas kernels: 85.6 us -> 76 us
  starting transfers between devices: 27.1 us -> 30.3 us
    pallas_call x2, Pallas kernels: 67.3 us -> 57.8 us  [beam_call(): pl.pallas_call(functools.partial(beam_kernel, plan), grid=(total_c // ct,...]
    ppermute x20, starting transfers between devices: 27.1 us -> 30.3 us  [swap(): return lax.ppermute(x, axis, [(i, i ^ mask) for i in range(size)])]
  transfers between devices with their start and end apart: 20 -> 20, of which waited for: 8 -> 8; matrix products, arithmetic and copies ran while one was open for 1% -> 1% of each run, Pallas kernels for 37% -> 35%
where the time goes in v2:
time: 135 us; the launch traced here: 134 us
  Pallas kernels  76 us (56%)
  starting transfers between devices  30.3 us (22%)
  waiting for transfers between devices  21.1 us (16%)
  local copies, waits for them, and re-layouts  4.92 us (4%)
  other arithmetic  1.96 us (1%)
    pallas_call x2, Pallas kernels, beam_call(): pl.pallas_call(functools.partial(beam_kernel, plan), grid=(total_c // ct,...  57.8 us
    ppermute x20, starting transfers between devices, swap(): return lax.ppermute(x, axis, [(i, i ^ mask) for i in range(size)])  30.3 us
    ppermute x20, waiting for transfers between devices, swap(): return lax.ppermute(x, axis, [(i, i ^ mask) for i in range(size)])  21.1 us
    pallas_call x2, Pallas kernels, steering(): pl.pallas_call(functools.partial(kernel, 1.0 / math.sqrt(total)), grid=(s...  18.2 us
  transfers between devices with their start and end apart: 20, of which 8 were waited for; matrix products, arithmetic and copies ran while one was open for 1% of the time, Pallas kernels for 35%

profile of v2, /device:TPU:0, one launch (start us, length us, event | category | flops | bytes accessed | tf_op | source)
XLA Modules:
  0.0 134.3 jit_solution(11954327545131381104)
XLA Ops:
  0.0 1.9 %fusion.8 = (bf16[2,96,1024]{2,1,0:T(8,128)(2,1)S(1)}, bf16[2,96,1024]{2,1,0:T(8,128)(2,1)}) fusion(bf16[2,96,2048]{2,1,0:T(8,128)(2,1)} %param.5), kind=kLoop, calls=%fused_computation.20 | loop fusion | bytes 1572864 | tf_op jit(solution)/shard_map/slice | solution.py:283
  1.9 3.0 %collective-permute-start.3 = (bf16[2,96,1024]{2,1,0:T(8,128)(2,1)}, bf16[2,96,1024]{2,1,0:T(8,128)(2,1)}, u32[]{:S(2)}, u32[]{:S(2)}) collective-permute-start(bf16[2,96,1024]{2,1,0:T(8,128)(2,1)} %get-tuple-element.25.refs_1_), channel_id=1, source_target_pairs={{0,8},{8,0},{16,24},{24,16},{1,9},{9,1},{17,25},{25,17},{2,10},{10... | collective-permute-start | bytes 1179656 | tf_op jit(solution)/shard_map/ppermute | solution.py:241
  4.9 1.5 %collective-permute-start = (bf16[2,48,4096]{2,1,0:T(8,128)(2,1)}, bf16[2,48,4096]{2,1,0:T(8,128)(2,1)}, u32[]{:S(2)}, u32[]{:S(2)}) collective-permute-start(bf16[2,48,4096]{2,1,0:T(8,128)(2,1)} %refs_5_.1), channel_id=1, source_target_pairs={{0,2},{1,3},{2,0},{3,1},{4,6},{5,7},{6,4},{7,5},{8,10},{9,11},{10,... | collective-permute-start | bytes 2359304 | tf_op jit(solution)/shard_map/ppermute | solution.py:241
  6.4 1.5 %collective-permute-start.1 = (bf16[2,48,4096]{2,1,0:T(8,128)(2,1)}, bf16[2,48,4096]{2,1,0:T(8,128)(2,1)}, u32[]{:S(2)}, u32[]{:S(2)}) collective-permute-start(bf16[2,48,4096]{2,1,0:T(8,128)(2,1)} %refs_5_.1), channel_id=1, source_target_pairs={{0,4},{1,5},{2,6},{3,7},{4,0},{5,1},{6,2},{7,3},{8,12},{9,13},{10,... | collective-permute-start | bytes 2359304 | tf_op jit(solution)/shard_map/ppermute | solution.py:241
  8.4 2.6 %collective-permute-start.4 = (bf16[2,96,1024]{2,1,0:T(8,128)(2,1)}, bf16[2,96,1024]{2,1,0:T(8,128)(2,1)}, u32[]{:S(2)}, u32[]{:S(2)}) collective-permute-start(bf16[2,96,1024]{2,1,0:T(8,128)(2,1)} %get-tuple-element.25.refs_1_), channel_id=1, source_target_pairs={{0,16},{8,24},{16,0},{24,8},{1,17},{9,25},{17,1},{25,9},{2,18},{10... | collective-permute-start | bytes 1179656 | tf_op jit(solution)/shard_map/ppermute | solution.py:241
  11.0 9.0 %collective-permute-done.3.refs_2_ = bf16[2,96,1024]{2,1,0:T(8,128)(2,1)} collective-permute-done((bf16[2,96,1024]{2,1,0:T(8,128)(2,1)}, bf16[2,96,1024]{2,1,0:T(8,128)(2,1)}, u32[]{:S(2)}, u32[]{:S(2)}) %collective-permute-start.3) | collective-permute-done | bytes 393248 | tf_op jit(solution)/shard_map/ppermute | solution.py:241
  20.0 2.6 %collective-permute-start.5 = (bf16[2,96,1024]{2,1,0:T(8,128)(2,1)}, bf16[2,96,1024]{2,1,0:T(8,128)(2,1)}, u32[]{:S(2)}, u32[]{:S(2)}) collective-permute-start(bf16[2,96,1024]{2,1,0:T(8,128)(2,1)} %get-tuple-element.25.refs_1_), channel_id=1, source_target_pairs={{0,24},{8,16},{16,8},{24,0},{1,25},{9,17},{17,9},{25,1},{2,26},{10... | collective-permute-start | bytes 1179656 | tf_op jit(solution)/shard_map/ppermute | solution.py:241
  22.7 7.3 %shard_map.47.refs_14_ = bf16[2048,768]{1,0:T(8,128)(2,1)} custom-call(f32[2048,384]{1,0:T(8,128)} %phase_ref.3), custom_call_target="tpu_custom_call" | custom-call | flops 7864 | bytes 7864 | tf_op jit(solution)/shard_map/pallas_call | solution.py:46
  30.0 10.9 %shard_map.46.refs_13_ = bf16[3,384,4096]{2,1,0:T(8,128)(2,1)} custom-call(f32[4096,384]{1,0:T(8,128)} %phase_ref.2), custom_call_target="tpu_custom_call" | custom-call | flops 15728 | bytes 15728 | tf_op jit(solution)/shard_map/pallas_call | solution.py:46
  40.9 1.4 %collective-permute-done.1.refs_7_ = bf16[2,48,4096]{2,1,0:T(8,128)(2,1)} collective-permute-done((bf16[2,48,4096]{2,1,0:T(8,128)(2,1)}, bf16[2,48,4096]{2,1,0:T(8,128)(2,1)}, u32[]{:S(2)}, u32[]{:S(2)}) %collective-permute-start.1) | collective-permute-done | bytes 786464 | tf_op jit(solution)/shard_map/ppermute | solution.py:241
  44.0 3.0 %collective-permute-start.6 = (bf16[2,96,1024]{2,1,0:T(8,128)(2,1)S(1)}, bf16[2,96,1024]{2,1,0:T(8,128)(2,1)}, u32[]{:S(2)}, u32[]{:S(2)}) collective-permute-start(bf16[2,96,1024]{2,1,0:T(8,128)(2,1)S(1)} %get-tuple-element.18.refs_1_), channel_id=1, source_target_pairs={{0,8},{8,0},{16,24},{24,16},{1,9},{9,1},{17,25},{25,17},{2,10},{10... | collective-permute-start | bytes 1179656 | tf_op jit(solution)/shard_map/ppermute | solution.py:241
  47.0 1.8 %collective-permute-start.7 = (bf16[2,96,1024]{2,1,0:T(8,128)(2,1)S(1)}, bf16[2,96,1024]{2,1,0:T(8,128)(2,1)}, u32[]{:S(2)}, u32[]{:S(2)}) collective-permute-start(bf16[2,96,1024]{2,1,0:T(8,128)(2,1)S(1)} %get-tuple-element.18.refs_1_), channel_id=1, source_target_pairs={{0,16},{8,24},{16,0},{24,8},{1,17},{9,25},{17,1},{25,9},{2,18},{10... | collective-permute-start | bytes 1179656 | tf_op jit(solution)/shard_map/ppermute | solution.py:241
  48.9 1.4 %collective-permute-start.8 = (bf16[2,96,1024]{2,1,0:T(8,128)(2,1)S(1)}, bf16[2,96,1024]{2,1,0:T(8,128)(2,1)}, u32[]{:S(2)}, u32[]{:S(2)}) collective-permute-start(bf16[2,96,1024]{2,1,0:T(8,128)(2,1)S(1)} %get-tuple-element.18.refs_1_), channel_id=1, source_target_pairs={{0,24},{8,16},{16,8},{24,0},{1,25},{9,17},{17,9},{25,1},{2,26},{10... | collective-permute-start | bytes 1179656 | tf_op jit(solution)/shard_map/ppermute | solution.py:241
  51.2 28.6 %shard_map.48.refs_15_ = f32[384,768]{1,0:T(8,128)} custom-call(s32[9]{0:T(128)} %stack.39.refs_0_, bf16[2,96,1024]{2,1,0:T(8,128)(2,1)} %get-tuple-element.25.refs_1_, bf16[2,96,1024]{2,1,0:T(8,128)(2,1)} %collective-permute-done.3.refs_2_, bf16[2,96,1024]{2,1,0:T(8,128)(2,1)} %collective-permute-done.4.refs_3_, ...), custom_call_target="tpu_custom_call" | custom-call | flops 20401094656 | bytes 16777216 | tf_op jit(solution)/shard_map/pallas_call | solution.py:217
  79.8 29.2 %shard_map.49 = (bf16[4,96,384]{2,1,0:T(8,128)(2,1)}, bf16[4,96,384]{2,1,0:T(8,128)(2,1)}) custom-call(s32[9]{0:T(128)} %stack.39.refs_0_, bf16[2,96,1024]{2,1,0:T(8,128)(2,1)} %copy-done, bf16[2,96,1024]{2,1,0:T(8,128)(2,1)} %collective-permute-done.6.refs_2_, bf16[2,96,1024]{2,1,0:T(8,128)(2,1)} %collective-permute-done.7.refs_3_, ...), custom_call_target="tpu_custom_call" | custom-call | flops 20401094656 | bytes 16777216 | tf_op jit(solution)/shard_map/pallas_call | solution.py:217
  109.1 1.8 %collective-permute-done.13 = bf16[4,96,384]{2,1,0:T(8,128)(2,1)S(1)} collective-permute-done((bf16[4,96,384]{2,1,0:T(8,128)(2,1)}, bf16[4,96,384]{2,1,0:T(8,128)(2,1)S(1)}, u32[]{:S(2)}, u32[]{:S(2)}) %collective-permute-start.13) | collective-permute-done | bytes 294944 | tf_op jit(solution)/shard_map/ppermute | solution.py:241
  111.9 1.6 %collective-permute-start.14 = (bf16[96,384]{1,0:T(8,128)(2,1)S(1)}, bf16[96,384]{1,0:T(8,128)(2,1)S(1)}, u32[]{:S(2)}, u32[]{:S(2)}) collective-permute-start(bf16[96,384]{1,0:T(8,128)(2,1)S(1)} %get-tuple-element.33), channel_id=1, source_target_pairs={{0,2},{1,3},{2,0},{3,1},{4,6},{5,7},{6,4},{7,5},{8,10},{9,11},{10,... | collective-permute-start | bytes 221192 | tf_op jit(solution)/shard_map/ppermute | solution.py:241
  113.5 1.5 %collective-permute-start.15 = (bf16[96,384]{1,0:T(8,128)(2,1)S(1)}, bf16[96,384]{1,0:T(8,128)(2,1)S(1)}, u32[]{:S(2)}, u32[]{:S(2)}) collective-permute-start(bf16[96,384]{1,0:T(8,128)(2,1)S(1)} %get-tuple-element.35), channel_id=1, source_target_pairs={{0,4},{1,5},{2,6},{3,7},{4,0},{5,1},{6,2},{7,3},{8,12},{9,13},{10,... | collective-permute-start | bytes 221192 | tf_op jit(solution)/shard_map/ppermute | solution.py:241
  116.3 1.5 %collective-permute-done.15 = bf16[96,384]{1,0:T(8,128)(2,1)S(1)} collective-permute-done((bf16[96,384]{1,0:T(8,128)(2,1)S(1)}, bf16[96,384]{1,0:T(8,128)(2,1)S(1)}, u32[]{:S(2)}, u32[]{:S(2)}) %collective-permute-start.15) | collective-permute-done | bytes 73760 | tf_op jit(solution)/shard_map/ppermute | solution.py:241
  117.8 2.4 %collective-permute-done.16 = bf16[96,384]{1,0:T(8,128)(2,1)S(1)} collective-permute-done((bf16[96,384]{1,0:T(8,128)(2,1)S(1)}, bf16[96,384]{1,0:T(8,128)(2,1)S(1)}, u32[]{:S(2)}, u32[]{:S(2)}) %collective-permute-start.16) | collective-permute-done | bytes 73760 | tf_op jit(solution)/shard_map/ppermute | solution.py:241
  121.6 5.0 %collective-permute-start.17 = (bf16[96,96]{1,0:T(8,128)(2,1)S(1)}, bf16[96,96]{1,0:T(8,128)(2,1)S(1)}, u32[]{:S(2)}, u32[]{:S(2)}) collective-permute-start(bf16[96,96]{1,0:T(8,128)(2,1)S(1)} %bitcast.43), channel_id=1, source_target_pairs={{0,8},{8,0},{16,24},{24,16},{1,9},{9,1},{17,25},{25,17},{2,10},{10... | collective-permute-start | bytes 55304 | tf_op jit(solution)/shard_map/ppermute | solution.py:241
  127.9 1.5 %collective-permute-start.19 = (bf16[96,96]{1,0:T(8,128)(2,1)S(1)}, bf16[96,96]{1,0:T(8,128)(2,1)S(1)}, u32[]{:S(2)}, u32[]{:S(2)}) collective-permute-start(bf16[96,96]{1,0:T(8,128)(2,1)S(1)} %bitcast.45), channel_id=1, source_target_pairs={{0,24},{8,16},{16,8},{24,0},{1,25},{9,17},{17,9},{25,1},{2,26},{10... | collective-permute-start | bytes 55304 | tf_op jit(solution)/shard_map/ppermute | solution.py:241
  129.6 2.0 %collective-permute-done.18 = bf16[96,96]{1,0:T(8,128)(2,1)S(1)} collective-permute-done((bf16[96,96]{1,0:T(8,128)(2,1)S(1)}, bf16[96,96]{1,0:T(8,128)(2,1)S(1)}, u32[]{:S(2)}, u32[]{:S(2)}) %collective-permute-start.18) | collective-permute-done | bytes 18464 | tf_op jit(solution)/shard_map/ppermute | solution.py:241
  131.6 2.0 %collective-permute-done.19 = bf16[96,96]{1,0:T(8,128)(2,1)S(1)} collective-permute-done((bf16[96,96]{1,0:T(8,128)(2,1)S(1)}, bf16[96,96]{1,0:T(8,128)(2,1)S(1)}, u32[]{:S(2)}, u32[]{:S(2)}) %collective-permute-start.19) | collective-permute-done | bytes 18464 | tf_op jit(solution)/shard_map/ppermute | solution.py:241
  (41 shorter events, 9.0 us)
Async XLA Ops:
  1.9 46.9 %copy-start = (bf16[2,96,1024]{2,1,0:T(8,128)(2,1)}, bf16[2,96,1024]{2,1,0:T(8,128)(2,1)S(1)}, u32[]{:S(2)}) copy-start(bf16[2,96,1024]{2,1,0:T(8,128)(2,1)S(1)} %get-tuple-element.18.refs_1_) | copy-start | bytes 1179652
  1.9 18.1 %collective-permute-start.3 = (bf16[2,96,1024]{2,1,0:T(8,128)(2,1)}, bf16[2,96,1024]{2,1,0:T(8,128)(2,1)}, u32[]{:S(2)}, u32[]{:S(2)}) collective-permute-start(bf16[2,96,1024]{2,1,0:T(8,128)(2,1)} %get-tuple-element.25.refs_1_), channel_id=1, source_target_pairs={{0,8},{8,0},{16,24},{24,16},{1,9},{9,1},{17,25},{25,17},{2,10},{10... | collective-permute-start | bytes 1179656 | tf_op jit(solution)/shard_map/ppermute | solution.py:241
  4.9 35.9 %collective-permute-start = (bf16[2,48,4096]{2,1,0:T(8,128)(2,1)}, bf16[2,48,4096]{2,1,0:T(8,128)(2,1)}, u32[]{:S(2)}, u32[]{:S(2)}) collective-permute-start(bf16[2,48,4096]{2,1,0:T(8,128)(2,1)} %refs_5_.1), channel_id=1, source_target_pairs={{0,2},{1,3},{2,0},{3,1},{4,6},{5,7},{6,4},{7,5},{8,10},{9,11},{10,... | collective-permute-start | bytes 2359304 | tf_op jit(solution)/shard_map/ppermute | solution.py:241
  6.4 35.9 %collective-permute-start.1 = (bf16[2,48,4096]{2,1,0:T(8,128)(2,1)}, bf16[2,48,4096]{2,1,0:T(8,128)(2,1)}, u32[]{:S(2)}, u32[]{:S(2)}) collective-permute-start(bf16[2,48,4096]{2,1,0:T(8,128)(2,1)} %refs_5_.1), channel_id=1, source_target_pairs={{0,4},{1,5},{2,6},{3,7},{4,0},{5,1},{6,2},{7,3},{8,12},{9,13},{10,... | collective-permute-start | bytes 2359304 | tf_op jit(solution)/shard_map/ppermute | solution.py:241
  8.0 34.4 %collective-permute-start.2 = (bf16[2,48,4096]{2,1,0:T(8,128)(2,1)}, bf16[2,48,4096]{2,1,0:T(8,128)(2,1)}, u32[]{:S(2)}, u32[]{:S(2)}) collective-permute-start(bf16[2,48,4096]{2,1,0:T(8,128)(2,1)} %refs_5_.1), channel_id=1, source_target_pairs={{0,6},{1,7},{2,4},{3,5},{4,2},{5,3},{6,0},{7,1},{8,14},{9,15},{10,... | collective-permute-start | bytes 2359304 | tf_op jit(solution)/shard_map/ppermute | solution.py:241
  8.4 32.4 %collective-permute-start.4 = (bf16[2,96,1024]{2,1,0:T(8,128)(2,1)}, bf16[2,96,1024]{2,1,0:T(8,128)(2,1)}, u32[]{:S(2)}, u32[]{:S(2)}) collective-permute-start(bf16[2,96,1024]{2,1,0:T(8,128)(2,1)} %get-tuple-element.25.refs_1_), channel_id=1, source_target_pairs={{0,16},{8,24},{16,0},{24,8},{1,17},{9,25},{17,1},{25,9},{2,18},{10... | collective-permute-start | bytes 1179656 | tf_op jit(solution)/shard_map/ppermute | solution.py:241
  20.0 20.9 %collective-permute-start.5 = (bf16[2,96,1024]{2,1,0:T(8,128)(2,1)}, bf16[2,96,1024]{2,1,0:T(8,128)(2,1)}, u32[]{:S(2)}, u32[]{:S(2)}) collective-permute-start(bf16[2,96,1024]{2,1,0:T(8,128)(2,1)} %get-tuple-element.25.refs_1_), channel_id=1, source_target_pairs={{0,24},{8,16},{16,8},{24,0},{1,25},{9,17},{17,9},{25,1},{2,26},{10... | collective-permute-start | bytes 1179656 | tf_op jit(solution)/shard_map/ppermute | solution.py:241
  42.3 4.7 %collective-permute-start.10 = (bf16[2,48,4096]{2,1,0:T(8,128)(2,1)}, bf16[2,48,4096]{2,1,0:T(8,128)(2,1)S(1)}, u32[]{:S(2)}, u32[]{:S(2)}) collective-permute-start(bf16[2,48,4096]{2,1,0:T(8,128)(2,1)} %collective-permute-done.refs_6_), channel_id=1, source_target_pairs={{0,1},{1,0},{2,3},{3,2},{4,5},{5,4},{6,7},{7,6},{8,9},{9,8},{10,11... | collective-permute-start | bytes 2359304 | tf_op jit(solution)/shard_map/ppermute | solution.py:241
  42.3 6.5 %collective-permute-start.11 = (bf16[2,48,4096]{2,1,0:T(8,128)(2,1)}, bf16[2,48,4096]{2,1,0:T(8,128)(2,1)S(1)}, u32[]{:S(2)}, u32[]{:S(2)}) collective-permute-start(bf16[2,48,4096]{2,1,0:T(8,128)(2,1)} %collective-permute-done.1.refs_7_), channel_id=1, source_target_pairs={{0,1},{1,0},{2,3},{3,2},{4,5},{5,4},{6,7},{7,6},{8,9},{9,8},{10,11... | collective-permute-start | bytes 2359304 | tf_op jit(solution)/shard_map/ppermute | solution.py:241
  42.8 7.4 %collective-permute-start.12 = (bf16[2,48,4096]{2,1,0:T(8,128)(2,1)}, bf16[2,48,4096]{2,1,0:T(8,128)(2,1)S(1)}, u32[]{:S(2)}, u32[]{:S(2)}) collective-permute-start(bf16[2,48,4096]{2,1,0:T(8,128)(2,1)} %collective-permute-done.2.refs_8_), channel_id=1, source_target_pairs={{0,1},{1,0},{2,3},{3,2},{4,5},{5,4},{6,7},{7,6},{8,9},{9,8},{10,11... | collective-permute-start | bytes 2359304 | tf_op jit(solution)/shard_map/ppermute | solution.py:241
  42.8 8.4 %collective-permute-start.9 = (bf16[2,48,4096]{2,1,0:T(8,128)(2,1)}, bf16[2,48,4096]{2,1,0:T(8,128)(2,1)}, u32[]{:S(2)}, u32[]{:S(2)}) collective-permute-start(bf16[2,48,4096]{2,1,0:T(8,128)(2,1)} %refs_5_.1), channel_id=1, source_target_pairs={{0,1},{1,0},{2,3},{3,2},{4,5},{5,4},{6,7},{7,6},{8,9},{9,8},{10,11... | collective-permute-start | bytes 2359304 | tf_op jit(solution)/shard_map/ppermute | solution.py:241
  44.0 35.8 %collective-permute-start.6 = (bf16[2,96,1024]{2,1,0:T(8,128)(2,1)S(1)}, bf16[2,96,1024]{2,1,0:T(8,128)(2,1)}, u32[]{:S(2)}, u32[]{:S(2)}) collective-permute-start(bf16[2,96,1024]{2,1,0:T(8,128)(2,1)S(1)} %get-tuple-element.18.refs_1_), channel_id=1, source_target_pairs={{0,8},{8,0},{16,24},{24,16},{1,9},{9,1},{17,25},{25,17},{2,10},{10... | collective-permute-start | bytes 1179656 | tf_op jit(solution)/shard_map/ppermute | solution.py:241
  47.0 3.2 %copy-start.1 = (bf16[2,48,4096]{2,1,0:T(8,128)(2,1)}, bf16[2,48,4096]{2,1,0:T(8,128)(2,1)S(1)}, u32[]{:S(2)}) copy-start(bf16[2,48,4096]{2,1,0:T(8,128)(2,1)S(1)} %collective-permute-done.10.refs_10_) | copy-start | bytes 2359300
  47.0 32.8 %collective-permute-start.7 = (bf16[2,96,1024]{2,1,0:T(8,128)(2,1)S(1)}, bf16[2,96,1024]{2,1,0:T(8,128)(2,1)}, u32[]{:S(2)}, u32[]{:S(2)}) collective-permute-start(bf16[2,96,1024]{2,1,0:T(8,128)(2,1)S(1)} %get-tuple-element.18.refs_1_), channel_id=1, source_target_pairs={{0,16},{8,24},{16,0},{24,8},{1,17},{9,25},{17,1},{25,9},{2,18},{10... | collective-permute-start | bytes 1179656 | tf_op jit(solution)/shard_map/ppermute | solution.py:241
  48.9 1.4 %copy-start.2 = (bf16[2,48,4096]{2,1,0:T(8,128)(2,1)}, bf16[2,48,4096]{2,1,0:T(8,128)(2,1)S(1)}, u32[]{:S(2)}) copy-start(bf16[2,48,4096]{2,1,0:T(8,128)(2,1)S(1)} %collective-permute-done.11.refs_11_) | copy-start | bytes 2359300
  48.9 30.9 %collective-permute-start.8 = (bf16[2,96,1024]{2,1,0:T(8,128)(2,1)S(1)}, bf16[2,96,1024]{2,1,0:T(8,128)(2,1)}, u32[]{:S(2)}, u32[]{:S(2)}) collective-permute-start(bf16[2,96,1024]{2,1,0:T(8,128)(2,1)S(1)} %get-tuple-element.18.refs_1_), channel_id=1, source_target_pairs={{0,24},{8,16},{16,8},{24,0},{1,25},{9,17},{17,9},{25,1},{2,26},{10... | collective-permute-start | bytes 1179656 | tf_op jit(solution)/shard_map/ppermute | solution.py:241
  50.3 0.9 copy-start.3
  109.1 1.9 %collective-permute-start.13 = (bf16[4,96,384]{2,1,0:T(8,128)(2,1)}, bf16[4,96,384]{2,1,0:T(8,128)(2,1)S(1)}, u32[]{:S(2)}, u32[]{:S(2)}) collective-permute-start(bf16[4,96,384]{2,1,0:T(8,128)(2,1)} %get-tuple-element.30), channel_id=1, source_target_pairs={{0,1},{1,0},{2,3},{3,2},{4,5},{5,4},{6,7},{7,6},{8,9},{9,8},{10,11... | collective-permute-start | bytes 884744 | tf_op jit(solution)/shard_map/ppermute | solution.py:241
  111.9 4.4 %collective-permute-start.14 = (bf16[96,384]{1,0:T(8,128)(2,1)S(1)}, bf16[96,384]{1,0:T(8,128)(2,1)S(1)}, u32[]{:S(2)}, u32[]{:S(2)}) collective-permute-start(bf16[96,384]{1,0:T(8,128)(2,1)S(1)} %get-tuple-element.33), channel_id=1, source_target_pairs={{0,2},{1,3},{2,0},{3,1},{4,6},{5,7},{6,4},{7,5},{8,10},{9,11},{10,... | collective-permute-start | bytes 221192 | tf_op jit(solution)/shard_map/ppermute | solution.py:241
  113.5 4.4 %collective-permute-start.15 = (bf16[96,384]{1,0:T(8,128)(2,1)S(1)}, bf16[96,384]{1,0:T(8,128)(2,1)S(1)}, u32[]{:S(2)}, u32[]{:S(2)}) collective-permute-start(bf16[96,384]{1,0:T(8,128)(2,1)S(1)} %get-tuple-element.35), channel_id=1, source_target_pairs={{0,4},{1,5},{2,6},{3,7},{4,0},{5,1},{6,2},{7,3},{8,12},{9,13},{10,... | collective-permute-start | bytes 221192 | tf_op jit(solution)/shard_map/ppermute | solution.py:241
  115.0 5.3 %collective-permute-start.16 = (bf16[96,384]{1,0:T(8,128)(2,1)S(1)}, bf16[96,384]{1,0:T(8,128)(2,1)S(1)}, u32[]{:S(2)}, u32[]{:S(2)}) collective-permute-start(bf16[96,384]{1,0:T(8,128)(2,1)S(1)} %get-tuple-element.34), channel_id=1, source_target_pairs={{0,6},{1,7},{2,4},{3,5},{4,2},{5,3},{6,0},{7,1},{8,14},{9,15},{10,... | collective-permute-start | bytes 221192 | tf_op jit(solution)/shard_map/ppermute | solution.py:241
  121.6 8.0 %collective-permute-start.17 = (bf16[96,96]{1,0:T(8,128)(2,1)S(1)}, bf16[96,96]{1,0:T(8,128)(2,1)S(1)}, u32[]{:S(2)}, u32[]{:S(2)}) collective-permute-start(bf16[96,96]{1,0:T(8,128)(2,1)S(1)} %bitcast.43), channel_id=1, source_target_pairs={{0,8},{8,0},{16,24},{24,16},{1,9},{9,1},{17,25},{25,17},{2,10},{10... | collective-permute-start | bytes 55304 | tf_op jit(solution)/shard_map/ppermute | solution.py:241
  126.7 4.8 %collective-permute-start.18 = (bf16[96,96]{1,0:T(8,128)(2,1)S(1)}, bf16[96,96]{1,0:T(8,128)(2,1)S(1)}, u32[]{:S(2)}, u32[]{:S(2)}) collective-permute-start(bf16[96,96]{1,0:T(8,128)(2,1)S(1)} %bitcast.44), channel_id=1, source_target_pairs={{0,16},{8,24},{16,0},{24,8},{1,17},{9,25},{17,1},{25,9},{2,18},{10... | collective-permute-start | bytes 55304 | tf_op jit(solution)/shard_map/ppermute | solution.py:241
  127.9 5.7 %collective-permute-start.19 = (bf16[96,96]{1,0:T(8,128)(2,1)S(1)}, bf16[96,96]{1,0:T(8,128)(2,1)S(1)}, u32[]{:S(2)}, u32[]{:S(2)}) collective-permute-start(bf16[96,96]{1,0:T(8,128)(2,1)S(1)} %bitcast.45), channel_id=1, source_target_pairs={{0,24},{8,16},{16,8},{24,0},{1,25},{9,17},{17,9},{25,1},{2,26},{10... | collective-permute-start | bytes 55304 | tf_op jit(solution)/shard_map/ppermute | solution.py:241

commit v3 on v2

--- a/solution.py
+++ b/solution.py
@@ -189,7 +189,7 @@
     n_a, total_c = csteer.shape[1:]
     n_b = rsteer.shape[1] // 2
     rc = r_pieces[0].shape[-1]
-    rows = min(1024, rc)
+    rows = rc if rc <= 1280 else 256
     ct = min(1024, total_c)
     wg, ws = split(windows)
     depth = wg + 2 * ws
@@ -247,7 +247,7 @@
     windows = n_rcv * height
     c = source_spectra.shape[2]
     r = receiver_spectra.shape[2]
-    fast = n_src == 4 and n_rcv == 8 and height % 16 == 0 and deep == 2 * height
+    fast = n_src == 4 and n_rcv == 8 and height % 16 == 0 and deep == 2 * height and r % 2048 == 0
     n_a = source_phase.shape[1]
     n_b = receiver_phase.shape[1]
     steps = 8
@@ -278,21 +278,32 @@
     places = [((2 * (z ^ mask) + h) ^ me) * height for mask in range(n_src) for h in (0, 1)]
     table = jnp.stack([me] + places).astype(jnp.int32)
     r_parts = (2,) * n_src
-    across, along, diagonal = [swap(source_spectra, "rcv", n_rcv, mask) for mask in (2, 4, 6)]
-    own = receiver_spectra[:, :, : r // 2]
-    own_b = receiver_spectra[:, :, r // 2 :]
-    r_first = [own] + [swap(own, "src", n_src, mask) for mask in range(1, n_src)]
+    cut = r // 2
+    own = receiver_spectra[:, :, :cut]
+    own_b = receiver_spectra[:, :, cut:]
+    across, along = [swap(source_spectra, "rcv", n_rcv, mask) for mask in (2, 4)]
+    mirror = swap(own, "src", n_src, 3)
+    near = swap(own, "src", n_src, 1)
     csteer = c_steering()
     rsteer = r_steering(receiver_phase)
-    s_pieces, r_first, csteer, rsteer, own_b = barrier(
-        ([source_spectra, across, along, diagonal], r_first, csteer, rsteer, own_b)
-    )
-    s_pieces += [swap(piece, "rcv", n_rcv, 1) for piece in s_pieces]
-    s_where = tuple((mask * height, (0, 1)) for mask in (0, 2, 4, 6, 1, 3, 5, 7))
+    across, along, mirror, near, own, own_b, csteer, rsteer, table = barrier(
+        (across, along, mirror, near, own, own_b, csteer, rsteer, table)
+    )
+    real = swap(along[:1], "rcv", n_rcv, 2)
+    imag = swap(across[1:], "rcv", n_rcv, 4)
+    passed = jnp.where(jnp.logical_or(z == 1, z == 2), mirror, own)
+    second = lax.ppermute(passed, "src", [(1, 0), (2, 3), (0, 2), (3, 1)])
+    early = [source_spectra, across, along]
+    early += [swap(piece, "rcv", n_rcv, 1) for piece in early]
+    real, imag, second, own_b = barrier((real, imag, second, own_b))
+    r_first = [own, near, second, mirror]
+    s_pieces = early + [real, imag] + [swap(piece, "rcv", n_rcv, 1) for piece in (real, imag)]
+    s_where = tuple((mask * height, (0, 1)) for mask in (0, 2, 4, 1, 3, 5))
+    s_where += tuple((mask * height, (plane,)) for mask in (6, 7) for plane in (0, 1))
     r_last = [own_b] + [swap(own_b, "src", n_src, mask) for mask in range(1, n_src)]
     (beams,) = beam_call(table, r_first, r_parts, s_pieces, s_where, csteer, rsteer, None, 0, windows, None)
     keep, send = beam_call(
-        table, r_last, r_parts, s_pieces, s_where, csteer, rsteer, beams, r // 2, windows, (n_rcv, True)
+        table, r_last, r_parts, s_pieces, s_where, csteer, rsteer, beams, cut, windows, (n_rcv, True)
     )
     got = swap(send, "rcv", n_rcv, 1)
     part = [keep[j].astype(F32) + got[j].astype(F32) for j in range(n_rcv // 2)]

time: 135 us -> 133 us (0.985)
  waiting for transfers between devices: 21.1 us -> 18.2 us
    ppermute x20 -> x21, waiting for transfers between devices: 21.1 us -> 12.5 us  [swap(): return lax.ppermute(x, axis, [(i, i ^ mask) for i in range(size)])]
    ppermute x0 -> x1, waiting for transfers between devices: none -> 5.72 us  [shards(): second = lax.ppermute(passed, 'src', [(1, 0), (2, 3), (0, 2), (3, 1)])]
    slice x1 -> x3, local copies, waits for them, and re-layouts: 1.91 us -> 3.97 us  [the longest x1 1.93 us: shards(): own_b = receiver_spectra[:, :, cut:]]
    ppermute x20 -> x21, starting transfers between devices: 30.3 us -> 28.2 us  [swap(): return lax.ppermute(x, axis, [(i, i ^ mask) for i in range(size)])]
    ppermute x0 -> x1, starting transfers between devices: none -> 1.82 us  [shards(): second = lax.ppermute(passed, 'src', [(1, 0), (2, 3), (0, 2), (3, 1)])]
  transfers between devices with their start and end apart: 20 -> 22, of which waited for: 8 -> 8; matrix products, arithmetic and copies ran while one was open for 1% -> 4% of each run, Pallas kernels for 35% -> 35%
where the time goes in v3:
time: 133 us
  Pallas kernels  76 us (57%)
  starting transfers between devices  30.1 us (23%)
  waiting for transfers between devices  18.2 us (14%)
  local copies, waits for them, and re-layouts  6.05 us (5%)
  other arithmetic  2.02 us (2%)
    pallas_call x2, Pallas kernels, beam_call(): pl.pallas_call(functools.partial(beam_kernel, plan), grid=(total_c // ct,...  57.8 us
    ppermute x21, starting transfers between devices, swap(): return lax.ppermute(x, axis, [(i, i ^ mask) for i in range(size)])  28.2 us
    pallas_call x2, Pallas kernels, steering(): pl.pallas_call(functools.partial(kernel, 1.0 / math.sqrt(total)), grid=(s...  18.2 us
    ppermute x21, waiting for transfers between devices, swap(): return lax.ppermute(x, axis, [(i, i ^ mask) for i in range(size)])  12.5 us
    ppermute x1, waiting for transfers between devices, shards(): second = lax.ppermute(passed, 'src', [(1, 0), (2, 3), (0, 2), (3, 1)])  5.72 us
  transfers between devices with their start and end apart: 22, of which 8 were waited for; matrix products, arithmetic and copies ran while one was open for 4% of the time, Pallas kernels for 35%

profile of v3, /device:TPU:0, one launch (start us, length us, event | category | flops | bytes accessed | tf_op | source)
XLA Modules:
  0.0 132.5 jit_solution(8979086002715773072)
XLA Ops:
  0.0 2.9 %collective-permute-start = (bf16[2,48,4096]{2,1,0:T(8,128)(2,1)}, bf16[2,48,4096]{2,1,0:T(8,128)(2,1)}, u32[]{:S(2)}, u32[]{:S(2)}) collective-permute-start(bf16[2,48,4096]{2,1,0:T(8,128)(2,1)} %refs_5_.3), channel_id=1, source_target_pairs={{0,2},{1,3},{2,0},{3,1},{4,6},{5,7},{6,4},{7,5},{8,10},{9,11},{10,... | collective-permute-start | bytes 2359304 | tf_op jit(solution)/shard_map/ppermute | solution.py:241
  2.9 1.5 %collective-permute-start.1 = (bf16[2,48,4096]{2,1,0:T(8,128)(2,1)}, bf16[2,48,4096]{2,1,0:T(8,128)(2,1)}, u32[]{:S(2)}, u32[]{:S(2)}) collective-permute-start(bf16[2,48,4096]{2,1,0:T(8,128)(2,1)} %refs_5_.3), channel_id=1, source_target_pairs={{0,4},{1,5},{2,6},{3,7},{4,0},{5,1},{6,2},{7,3},{8,12},{9,13},{10,... | collective-permute-start | bytes 2359304 | tf_op jit(solution)/shard_map/ppermute | solution.py:241
  4.5 1.9 %fusion.8 = (bf16[2,96,1024]{2,1,0:T(8,128)(2,1)}, bf16[2,96,1024]{2,1,0:T(8,128)(2,1)S(1)}) fusion(bf16[2,96,2048]{2,1,0:T(8,128)(2,1)} %param.5), kind=kLoop, calls=%fused_computation.21 | loop fusion | bytes 1572864 | tf_op jit(solution)/shard_map/slice | solution.py:283
  6.4 3.6 %collective-permute-start.2 = (bf16[2,96,1024]{2,1,0:T(8,128)(2,1)S(1)}, bf16[2,96,1024]{2,1,0:T(8,128)(2,1)}, u32[]{:S(2)}, u32[]{:S(2)}) collective-permute-start(bf16[2,96,1024]{2,1,0:T(8,128)(2,1)S(1)} %get-tuple-element.24.refs_1_), channel_id=1, source_target_pairs={{0,24},{8,16},{16,8},{24,0},{1,25},{9,17},{17,9},{25,1},{2,26},{10... | collective-permute-start | bytes 1179656 | tf_op jit(solution)/shard_map/ppermute | solution.py:241
  10.0 7.3 %shard_map.47.refs_16_ = bf16[2048,768]{1,0:T(8,128)(2,1)} custom-call(f32[2048,384]{1,0:T(8,128)} %phase_ref.3), custom_call_target="tpu_custom_call" | custom-call | flops 7864 | bytes 7864 | tf_op jit(solution)/shard_map/pallas_call | solution.py:46
  17.3 10.9 %shard_map.46.refs_15_ = bf16[3,384,4096]{2,1,0:T(8,128)(2,1)} custom-call(f32[4096,384]{1,0:T(8,128)} %phase_ref.2), custom_call_target="tpu_custom_call" | custom-call | flops 15728 | bytes 15728 | tf_op jit(solution)/shard_map/pallas_call | solution.py:46
  28.9 1.8 %collective-permute-start.6 = (bf16[2,96,1024]{2,1,0:T(8,128)(2,1)S(1)}, bf16[2,96,1024]{2,1,0:T(8,128)(2,1)S(1)}, u32[]{:S(2)}, u32[]{:S(2)}) collective-permute-start(bf16[2,96,1024]{2,1,0:T(8,128)(2,1)S(1)} %broadcast_select_fusion), channel_id=1, source_target_pairs={{8,0},{16,24},{0,16},{24,8},{9,1},{17,25},{1,17},{25,9},{10,2},{18... | collective-permute-start | bytes 1179656 | tf_op jit(solution)/shard_map/ppermute | solution.py:295
  34.2 5.7 %collective-permute-done.6.refs_3_ = bf16[2,96,1024]{2,1,0:T(8,128)(2,1)S(1)} collective-permute-done((bf16[2,96,1024]{2,1,0:T(8,128)(2,1)S(1)}, bf16[2,96,1024]{2,1,0:T(8,128)(2,1)S(1)}, u32[]{:S(2)}, u32[]{:S(2)}) %collective-permute-start.6) | collective-permute-done | bytes 393248 | tf_op jit(solution)/shard_map/ppermute | solution.py:295
  40.0 1.4 %collective-permute-done.4.refs_11_ = bf16[1,48,4096]{2,1,0:T(8,128)(2,1)S(1)} collective-permute-done((bf16[1,48,4096]{2,1,0:T(8,128)(2,1)S(1)}, bf16[1,48,4096]{2,1,0:T(8,128)(2,1)S(1)}, u32[]{:S(2)}, u32[]{:S(2)}) %collective-permute-start.4) | collective-permute-done | bytes 393248 | tf_op jit(solution)/shard_map/ppermute | solution.py:241
  41.3 1.3 %collective-permute-done.5.refs_12_ = bf16[1,48,4096]{2,1,0:T(8,128)(2,1)S(1)} collective-permute-done((bf16[1,48,4096]{2,1,0:T(8,128)(2,1)S(1)}, bf16[1,48,4096]{2,1,0:T(8,128)(2,1)S(1)}, u32[]{:S(2)}, u32[]{:S(2)}) %collective-permute-start.5) | collective-permute-done | bytes 393248 | tf_op jit(solution)/shard_map/ppermute | solution.py:241
  43.2 1.5 %collective-permute-start.7 = (bf16[2,96,1024]{2,1,0:T(8,128)(2,1)}, bf16[2,96,1024]{2,1,0:T(8,128)(2,1)}, u32[]{:S(2)}, u32[]{:S(2)}) collective-permute-start(bf16[2,96,1024]{2,1,0:T(8,128)(2,1)} %get-tuple-element.26.refs_1_), channel_id=1, source_target_pairs={{0,8},{8,0},{16,24},{24,16},{1,9},{9,1},{17,25},{25,17},{2,10},{10... | collective-permute-start | bytes 1179656 | tf_op jit(solution)/shard_map/ppermute | solution.py:241
  44.7 2.7 %collective-permute-start.8 = (bf16[2,96,1024]{2,1,0:T(8,128)(2,1)}, bf16[2,96,1024]{2,1,0:T(8,128)(2,1)}, u32[]{:S(2)}, u32[]{:S(2)}) collective-permute-start(bf16[2,96,1024]{2,1,0:T(8,128)(2,1)} %get-tuple-element.26.refs_1_), channel_id=1, source_target_pairs={{0,16},{8,24},{16,0},{24,8},{1,17},{9,25},{17,1},{25,9},{2,18},{10... | collective-permute-start | bytes 1179656 | tf_op jit(solution)/shard_map/ppermute | solution.py:241
  47.4 1.1 collective-permute-start.9
  48.5 28.6 %shard_map.48.refs_17_ = f32[384,768]{1,0:T(8,128)} custom-call(s32[9]{0:T(128)} %stack.39.refs_0_, bf16[2,96,1024]{2,1,0:T(8,128)(2,1)} %copy-done, bf16[2,96,1024]{2,1,0:T(8,128)(2,1)} %collective-permute-done.3.refs_2_, bf16[2,96,1024]{2,1,0:T(8,128)(2,1)} %copy-done.3, bf16[2,96,1024]{2,1,0:T(8,128)(2,1)} %collective-permute-done.2.refs_4_, ...), custom_call_target="tpu_custom_call" | custom-call | flops 20401094656 | bytes 16777216 | tf_op jit(solution)/shard_map/pallas_call | solution.py:217
  77.1 29.3 %shard_map.49 = (bf16[4,96,384]{2,1,0:T(8,128)(2,1)}, bf16[4,96,384]{2,1,0:T(8,128)(2,1)}) custom-call(s32[9]{0:T(128)} %stack.39.refs_0_, bf16[2,96,1024]{2,1,0:T(8,128)(2,1)} %get-tuple-element.26.refs_1_, bf16[2,96,1024]{2,1,0:T(8,128)(2,1)} %collective-permute-done.7.refs_2_, bf16[2,96,1024]{2,1,0:T(8,128)(2,1)} %collective-permute-done.8.refs_3_, ...), custom_call_target="tpu_custom_call" | custom-call | flops 20401094656 | bytes 16777216 | tf_op jit(solution)/shard_map/pallas_call | solution.py:217
  106.5 1.8 %collective-permute-done.15 = bf16[4,96,384]{2,1,0:T(8,128)(2,1)S(1)} collective-permute-done((bf16[4,96,384]{2,1,0:T(8,128)(2,1)}, bf16[4,96,384]{2,1,0:T(8,128)(2,1)S(1)}, u32[]{:S(2)}, u32[]{:S(2)}) %collective-permute-start.15) | collective-permute-done | bytes 294944 | tf_op jit(solution)/shard_map/ppermute | solution.py:241
  109.3 1.6 %collective-permute-start.16 = (bf16[96,384]{1,0:T(8,128)(2,1)S(1)}, bf16[96,384]{1,0:T(8,128)(2,1)S(1)}, u32[]{:S(2)}, u32[]{:S(2)}) collective-permute-start(bf16[96,384]{1,0:T(8,128)(2,1)S(1)} %get-tuple-element.37), channel_id=1, source_target_pairs={{0,2},{1,3},{2,0},{3,1},{4,6},{5,7},{6,4},{7,5},{8,10},{9,11},{10,... | collective-permute-start | bytes 221192 | tf_op jit(solution)/shard_map/ppermute | solution.py:241
  111.4 1.5 %collective-permute-start.18 = (bf16[96,384]{1,0:T(8,128)(2,1)S(1)}, bf16[96,384]{1,0:T(8,128)(2,1)S(1)}, u32[]{:S(2)}, u32[]{:S(2)}) collective-permute-start(bf16[96,384]{1,0:T(8,128)(2,1)S(1)} %get-tuple-element.38), channel_id=1, source_target_pairs={{0,6},{1,7},{2,4},{3,5},{4,2},{5,3},{6,0},{7,1},{8,14},{9,15},{10,... | collective-permute-start | bytes 221192 | tf_op jit(solution)/shard_map/ppermute | solution.py:241
  113.7 3.1 %collective-permute-done.17 = bf16[96,384]{1,0:T(8,128)(2,1)S(1)} collective-permute-done((bf16[96,384]{1,0:T(8,128)(2,1)S(1)}, bf16[96,384]{1,0:T(8,128)(2,1)S(1)}, u32[]{:S(2)}, u32[]{:S(2)}) %collective-permute-start.17) | collective-permute-done | bytes 73760 | tf_op jit(solution)/shard_map/ppermute | solution.py:241
  118.2 5.7 %collective-permute-start.19 = (bf16[96,96]{1,0:T(8,128)(2,1)S(1)}, bf16[96,96]{1,0:T(8,128)(2,1)S(1)}, u32[]{:S(2)}, u32[]{:S(2)}) collective-permute-start(bf16[96,96]{1,0:T(8,128)(2,1)S(1)} %bitcast.43), channel_id=1, source_target_pairs={{0,8},{8,0},{16,24},{24,16},{1,9},{9,1},{17,25},{25,17},{2,10},{10... | collective-permute-start | bytes 55304 | tf_op jit(solution)/shard_map/ppermute | solution.py:241
  124.0 2.0 %collective-permute-start.20 = (bf16[96,96]{1,0:T(8,128)(2,1)S(1)}, bf16[96,96]{1,0:T(8,128)(2,1)S(1)}, u32[]{:S(2)}, u32[]{:S(2)}) collective-permute-start(bf16[96,96]{1,0:T(8,128)(2,1)S(1)} %bitcast.44), channel_id=1, source_target_pairs={{0,16},{8,24},{16,0},{24,8},{1,17},{9,25},{17,1},{25,9},{2,18},{10... | collective-permute-start | bytes 55304 | tf_op jit(solution)/shard_map/ppermute | solution.py:241
  126.1 1.5 %collective-permute-start.21 = (bf16[96,96]{1,0:T(8,128)(2,1)S(1)}, bf16[96,96]{1,0:T(8,128)(2,1)S(1)}, u32[]{:S(2)}, u32[]{:S(2)}) collective-permute-start(bf16[96,96]{1,0:T(8,128)(2,1)S(1)} %bitcast.45), channel_id=1, source_target_pairs={{0,24},{8,16},{16,8},{24,0},{1,25},{9,17},{17,9},{25,1},{2,26},{10... | collective-permute-start | bytes 55304 | tf_op jit(solution)/shard_map/ppermute | solution.py:241
  127.8 1.3 collective-permute-done.20
  129.1 2.7 %collective-permute-done.21 = bf16[96,96]{1,0:T(8,128)(2,1)S(1)} collective-permute-done((bf16[96,96]{1,0:T(8,128)(2,1)S(1)}, bf16[96,96]{1,0:T(8,128)(2,1)S(1)}, u32[]{:S(2)}, u32[]{:S(2)}) %collective-permute-start.21) | collective-permute-done | bytes 18464 | tf_op jit(solution)/shard_map/ppermute | solution.py:241
  (52 shorter events, 9.6 us)
Async XLA Ops:
  0.0 28.8 %collective-permute-start = (bf16[2,48,4096]{2,1,0:T(8,128)(2,1)}, bf16[2,48,4096]{2,1,0:T(8,128)(2,1)}, u32[]{:S(2)}, u32[]{:S(2)}) collective-permute-start(bf16[2,48,4096]{2,1,0:T(8,128)(2,1)} %refs_5_.3), channel_id=1, source_target_pairs={{0,2},{1,3},{2,0},{3,1},{4,6},{5,7},{6,4},{7,5},{8,10},{9,11},{10,... | collective-permute-start | bytes 2359304 | tf_op jit(solution)/shard_map/ppermute | solution.py:241
  2.9 25.9 %collective-permute-start.1 = (bf16[2,48,4096]{2,1,0:T(8,128)(2,1)}, bf16[2,48,4096]{2,1,0:T(8,128)(2,1)}, u32[]{:S(2)}, u32[]{:S(2)}) collective-permute-start(bf16[2,48,4096]{2,1,0:T(8,128)(2,1)} %refs_5_.3), channel_id=1, source_target_pairs={{0,4},{1,5},{2,6},{3,7},{4,0},{5,1},{6,2},{7,3},{8,12},{9,13},{10,... | collective-permute-start | bytes 2359304 | tf_op jit(solution)/shard_map/ppermute | solution.py:241
  6.4 22.4 %copy-start = (bf16[2,96,1024]{2,1,0:T(8,128)(2,1)}, bf16[2,96,1024]{2,1,0:T(8,128)(2,1)S(1)}, u32[]{:S(2)}) copy-start(bf16[2,96,1024]{2,1,0:T(8,128)(2,1)S(1)} %get-tuple-element.24.refs_1_) | copy-start | bytes 1179652
  6.4 22.4 %collective-permute-start.2 = (bf16[2,96,1024]{2,1,0:T(8,128)(2,1)S(1)}, bf16[2,96,1024]{2,1,0:T(8,128)(2,1)}, u32[]{:S(2)}, u32[]{:S(2)}) collective-permute-start(bf16[2,96,1024]{2,1,0:T(8,128)(2,1)S(1)} %get-tuple-element.24.refs_1_), channel_id=1, source_target_pairs={{0,24},{8,16},{16,8},{24,0},{1,25},{9,17},{17,9},{25,1},{2,26},{10... | collective-permute-start | bytes 1179656 | tf_op jit(solution)/shard_map/ppermute | solution.py:241
  10.0 18.8 %collective-permute-start.3 = (bf16[2,96,1024]{2,1,0:T(8,128)(2,1)S(1)}, bf16[2,96,1024]{2,1,0:T(8,128)(2,1)}, u32[]{:S(2)}, u32[]{:S(2)}) collective-permute-start(bf16[2,96,1024]{2,1,0:T(8,128)(2,1)S(1)} %get-tuple-element.24.refs_1_), channel_id=1, source_target_pairs={{0,8},{8,0},{16,24},{24,16},{1,9},{9,1},{17,25},{25,17},{2,10},{10... | collective-permute-start | bytes 1179656 | tf_op jit(solution)/shard_map/ppermute | solution.py:241
  28.9 11.1 %collective-permute-start.6 = (bf16[2,96,1024]{2,1,0:T(8,128)(2,1)S(1)}, bf16[2,96,1024]{2,1,0:T(8,128)(2,1)S(1)}, u32[]{:S(2)}, u32[]{:S(2)}) collective-permute-start(bf16[2,96,1024]{2,1,0:T(8,128)(2,1)S(1)} %broadcast_select_fusion), channel_id=1, source_target_pairs={{8,0},{16,24},{0,16},{24,8},{9,1},{17,25},{1,17},{25,9},{10,2},{18... | collective-permute-start | bytes 1179656 | tf_op jit(solution)/shard_map/ppermute | solution.py:295
  31.8 9.6 %collective-permute-start.4 = (bf16[1,48,4096]{2,1,0:T(8,128)(2,1)S(1)}, bf16[1,48,4096]{2,1,0:T(8,128)(2,1)S(1)}, u32[]{:S(2)}, u32[]{:S(2)}) collective-permute-start(bf16[1,48,4096]{2,1,0:T(8,128)(2,1)S(1)} %slice.38), channel_id=1, source_target_pairs={{0,2},{1,3},{2,0},{3,1},{4,6},{5,7},{6,4},{7,5},{8,10},{9,11},{10,... | collective-permute-start | bytes 1179656 | tf_op jit(solution)/shard_map/ppermute | solution.py:241
  33.4 9.3 %collective-permute-start.5 = (bf16[1,48,4096]{2,1,0:T(8,128)(2,1)S(1)}, bf16[1,48,4096]{2,1,0:T(8,128)(2,1)S(1)}, u32[]{:S(2)}, u32[]{:S(2)}) collective-permute-start(bf16[1,48,4096]{2,1,0:T(8,128)(2,1)S(1)} %slice.39), channel_id=1, source_target_pairs={{0,4},{1,5},{2,6},{3,7},{4,0},{5,1},{6,2},{7,3},{8,12},{9,13},{10,... | collective-permute-start | bytes 1179656 | tf_op jit(solution)/shard_map/ppermute | solution.py:241
  33.7 9.5 %collective-permute-start.10 = (bf16[2,48,4096]{2,1,0:T(8,128)(2,1)}, bf16[2,48,4096]{2,1,0:T(8,128)(2,1)}, u32[]{:S(2)}, u32[]{:S(2)}) collective-permute-start(bf16[2,48,4096]{2,1,0:T(8,128)(2,1)} %refs_5_.3), channel_id=1, source_target_pairs={{0,1},{1,0},{2,3},{3,2},{4,5},{5,4},{6,7},{7,6},{8,9},{9,8},{10,11... | collective-permute-start | bytes 2359304 | tf_op jit(solution)/shard_map/ppermute | solution.py:241
  33.7 14.8 %collective-permute-start.11 = (bf16[2,48,4096]{2,1,0:T(8,128)(2,1)}, bf16[2,48,4096]{2,1,0:T(8,128)(2,1)}, u32[]{:S(2)}, u32[]{:S(2)}) collective-permute-start(bf16[2,48,4096]{2,1,0:T(8,128)(2,1)} %collective-permute-done.refs_6_), channel_id=1, source_target_pairs={{0,1},{1,0},{2,3},{3,2},{4,5},{5,4},{6,7},{7,6},{8,9},{9,8},{10,11... | collective-permute-start | bytes 2359304 | tf_op jit(solution)/shard_map/ppermute | solution.py:241
  40.0 7.4 %copy-start.3 = (bf16[2,96,1024]{2,1,0:T(8,128)(2,1)}, bf16[2,96,1024]{2,1,0:T(8,128)(2,1)S(1)}, u32[]{:S(2)}) copy-start(bf16[2,96,1024]{2,1,0:T(8,128)(2,1)S(1)} %collective-permute-done.6.refs_3_) | copy-start | bytes 1179652
  40.0 8.6 %collective-permute-start.12 = (bf16[2,48,4096]{2,1,0:T(8,128)(2,1)}, bf16[2,48,4096]{2,1,0:T(8,128)(2,1)}, u32[]{:S(2)}, u32[]{:S(2)}) collective-permute-start(bf16[2,48,4096]{2,1,0:T(8,128)(2,1)} %collective-permute-done.1.refs_7_), channel_id=1, source_target_pairs={{0,1},{1,0},{2,3},{3,2},{4,5},{5,4},{6,7},{7,6},{8,9},{9,8},{10,11... | collective-permute-start | bytes 2359304 | tf_op jit(solution)/shard_map/ppermute | solution.py:241
  42.7 2.0 %collective-permute-start.13 = (bf16[1,48,4096]{2,1,0:T(8,128)(2,1)S(1)}, bf16[1,48,4096]{2,1,0:T(8,128)(2,1)S(1)}, u32[]{:S(2)}, u32[]{:S(2)}) collective-permute-start(bf16[1,48,4096]{2,1,0:T(8,128)(2,1)S(1)} %collective-permute-done.4.refs_11_), channel_id=1, source_target_pairs={{0,1},{1,0},{2,3},{3,2},{4,5},{5,4},{6,7},{7,6},{8,9},{9,8},{10,11... | collective-permute-start | bytes 1179656 | tf_op jit(solution)/shard_map/ppermute | solution.py:241
  42.7 4.7 %collective-permute-start.14 = (bf16[1,48,4096]{2,1,0:T(8,128)(2,1)S(1)}, bf16[1,48,4096]{2,1,0:T(8,128)(2,1)S(1)}, u32[]{:S(2)}, u32[]{:S(2)}) collective-permute-start(bf16[1,48,4096]{2,1,0:T(8,128)(2,1)S(1)} %collective-permute-done.5.refs_12_), channel_id=1, source_target_pairs={{0,1},{1,0},{2,3},{3,2},{4,5},{5,4},{6,7},{7,6},{8,9},{9,8},{10,11... | collective-permute-start | bytes 1179656 | tf_op jit(solution)/shard_map/ppermute | solution.py:241
  43.2 33.9 %collective-permute-start.7 = (bf16[2,96,1024]{2,1,0:T(8,128)(2,1)}, bf16[2,96,1024]{2,1,0:T(8,128)(2,1)}, u32[]{:S(2)}, u32[]{:S(2)}) collective-permute-start(bf16[2,96,1024]{2,1,0:T(8,128)(2,1)} %get-tuple-element.26.refs_1_), channel_id=1, source_target_pairs={{0,8},{8,0},{16,24},{24,16},{1,9},{9,1},{17,25},{25,17},{2,10},{10... | collective-permute-start | bytes 1179656 | tf_op jit(solution)/shard_map/ppermute | solution.py:241
  44.7 32.4 %collective-permute-start.8 = (bf16[2,96,1024]{2,1,0:T(8,128)(2,1)}, bf16[2,96,1024]{2,1,0:T(8,128)(2,1)}, u32[]{:S(2)}, u32[]{:S(2)}) collective-permute-start(bf16[2,96,1024]{2,1,0:T(8,128)(2,1)} %get-tuple-element.26.refs_1_), channel_id=1, source_target_pairs={{0,16},{8,24},{16,0},{24,8},{1,17},{9,25},{17,1},{25,9},{2,18},{10... | collective-permute-start | bytes 1179656 | tf_op jit(solution)/shard_map/ppermute | solution.py:241
  47.4 29.8 %collective-permute-start.9 = (bf16[2,96,1024]{2,1,0:T(8,128)(2,1)}, bf16[2,96,1024]{2,1,0:T(8,128)(2,1)}, u32[]{:S(2)}, u32[]{:S(2)}) collective-permute-start(bf16[2,96,1024]{2,1,0:T(8,128)(2,1)} %get-tuple-element.26.refs_1_), channel_id=1, source_target_pairs={{0,24},{8,16},{16,8},{24,0},{1,25},{9,17},{17,9},{25,1},{2,26},{10... | collective-permute-start | bytes 1179656 | tf_op jit(solution)/shard_map/ppermute | solution.py:241
  106.4 1.9 %collective-permute-start.15 = (bf16[4,96,384]{2,1,0:T(8,128)(2,1)}, bf16[4,96,384]{2,1,0:T(8,128)(2,1)S(1)}, u32[]{:S(2)}, u32[]{:S(2)}) collective-permute-start(bf16[4,96,384]{2,1,0:T(8,128)(2,1)} %get-tuple-element.34), channel_id=1, source_target_pairs={{0,1},{1,0},{2,3},{3,2},{4,5},{5,4},{6,7},{7,6},{8,9},{9,8},{10,11... | collective-permute-start | bytes 884744 | tf_op jit(solution)/shard_map/ppermute | solution.py:241
  109.3 4.4 %collective-permute-start.16 = (bf16[96,384]{1,0:T(8,128)(2,1)S(1)}, bf16[96,384]{1,0:T(8,128)(2,1)S(1)}, u32[]{:S(2)}, u32[]{:S(2)}) collective-permute-start(bf16[96,384]{1,0:T(8,128)(2,1)S(1)} %get-tuple-element.37), channel_id=1, source_target_pairs={{0,2},{1,3},{2,0},{3,1},{4,6},{5,7},{6,4},{7,5},{8,10},{9,11},{10,... | collective-permute-start | bytes 221192 | tf_op jit(solution)/shard_map/ppermute | solution.py:241
  110.9 5.9 %collective-permute-start.17 = (bf16[96,384]{1,0:T(8,128)(2,1)S(1)}, bf16[96,384]{1,0:T(8,128)(2,1)S(1)}, u32[]{:S(2)}, u32[]{:S(2)}) collective-permute-start(bf16[96,384]{1,0:T(8,128)(2,1)S(1)} %get-tuple-element.39), channel_id=1, source_target_pairs={{0,4},{1,5},{2,6},{3,7},{4,0},{5,1},{6,2},{7,3},{8,12},{9,13},{10,... | collective-permute-start | bytes 221192 | tf_op jit(solution)/shard_map/ppermute | solution.py:241
  111.4 5.4 %collective-permute-start.18 = (bf16[96,384]{1,0:T(8,128)(2,1)S(1)}, bf16[96,384]{1,0:T(8,128)(2,1)S(1)}, u32[]{:S(2)}, u32[]{:S(2)}) collective-permute-start(bf16[96,384]{1,0:T(8,128)(2,1)S(1)} %get-tuple-element.38), channel_id=1, source_target_pairs={{0,6},{1,7},{2,4},{3,5},{4,2},{5,3},{6,0},{7,1},{8,14},{9,15},{10,... | collective-permute-start | bytes 221192 | tf_op jit(solution)/shard_map/ppermute | solution.py:241
  118.2 9.6 %collective-permute-start.19 = (bf16[96,96]{1,0:T(8,128)(2,1)S(1)}, bf16[96,96]{1,0:T(8,128)(2,1)S(1)}, u32[]{:S(2)}, u32[]{:S(2)}) collective-permute-start(bf16[96,96]{1,0:T(8,128)(2,1)S(1)} %bitcast.43), channel_id=1, source_target_pairs={{0,8},{8,0},{16,24},{24,16},{1,9},{9,1},{17,25},{25,17},{2,10},{10... | collective-permute-start | bytes 55304 | tf_op jit(solution)/shard_map/ppermute | solution.py:241
  124.0 5.1 %collective-permute-start.20 = (bf16[96,96]{1,0:T(8,128)(2,1)S(1)}, bf16[96,96]{1,0:T(8,128)(2,1)S(1)}, u32[]{:S(2)}, u32[]{:S(2)}) collective-permute-start(bf16[96,96]{1,0:T(8,128)(2,1)S(1)} %bitcast.44), channel_id=1, source_target_pairs={{0,16},{8,24},{16,0},{24,8},{1,17},{9,25},{17,1},{25,9},{2,18},{10... | collective-permute-start | bytes 55304 | tf_op jit(solution)/shard_map/ppermute | solution.py:241
  126.1 5.7 %collective-permute-start.21 = (bf16[96,96]{1,0:T(8,128)(2,1)S(1)}, bf16[96,96]{1,0:T(8,128)(2,1)S(1)}, u32[]{:S(2)}, u32[]{:S(2)}) collective-permute-start(bf16[96,96]{1,0:T(8,128)(2,1)S(1)} %bitcast.45), channel_id=1, source_target_pairs={{0,24},{8,16},{16,8},{24,0},{1,25},{9,17},{17,9},{25,1},{2,26},{10... | collective-permute-start | bytes 55304 | tf_op jit(solution)/shard_map/ppermute | solution.py:241
  (4 other events, 14.2 us)

commit v4 on v3

--- a/solution.py
+++ b/solution.py
@@ -295,7 +295,7 @@
     second = lax.ppermute(passed, "src", [(1, 0), (2, 3), (0, 2), (3, 1)])
     early = [source_spectra, across, along]
     early += [swap(piece, "rcv", n_rcv, 1) for piece in early]
-    real, imag, second, own_b = barrier((real, imag, second, own_b))
+    second, own_b = barrier((second, own_b))
     r_first = [own, near, second, mirror]
     s_pieces = early + [real, imag] + [swap(piece, "rcv", n_rcv, 1) for piece in (real, imag)]
     s_where = tuple((mask * height, (0, 1)) for mask in (0, 2, 4, 1, 3, 5))

time: 133 us -> 135 us (1.015)
  waiting for transfers between devices: 18.2 us -> 20.7 us
    ppermute x21, waiting for transfers between devices: 12.5 us -> 19.1 us  [swap(): return lax.ppermute(x, axis, [(i, i ^ mask) for i in range(size)])]
    ppermute x1, waiting for transfers between devices: 5.72 us -> 1.6 us  [shards(): second = lax.ppermute(passed, 'src', [(1, 0), (2, 3), (0, 2), (3, 1)])]
  transfers between devices with their start and end apart: 22 -> 22, of which waited for: 8 -> 9; matrix products, arithmetic and copies ran while one was open for 4% -> 3% of each run, Pallas kernels for 35% -> 35%
where the time goes in v4:
time: 135 us; the launch traced here: 134 us
  Pallas kernels  76 us (56%)
  starting transfers between devices  29.4 us (22%)
  waiting for transfers between devices  20.7 us (15%)
  local copies, waits for them, and re-layouts  6.06 us (4%)
  other arithmetic  2.01 us (1%)
    pallas_call x2, Pallas kernels, beam_call(): pl.pallas_call(functools.partial(beam_kernel, plan), grid=(total_c // ct,...  57.8 us
    ppermute x21, starting transfers between devices, swap(): return lax.ppermute(x, axis, [(i, i ^ mask) for i in range(size)])  27.8 us
    ppermute x21, waiting for transfers between devices, swap(): return lax.ppermute(x, axis, [(i, i ^ mask) for i in range(size)])  19.1 us
    pallas_call x2, Pallas kernels, steering(): pl.pallas_call(functools.partial(kernel, 1.0 / math.sqrt(total)), grid=(s...  18.2 us
  transfers between devices with their start and end apart: 22, of which 9 were waited for; matrix products, arithmetic and copies ran while one was open for 3% of the time, Pallas kernels for 35%

profile of v4, /device:TPU:0, one launch (start us, length us, event | category | flops | bytes accessed | tf_op | source)
XLA Modules:
  0.0 134.4 jit_solution(10125869482004952639)
XLA Ops:
  0.0 2.9 %collective-permute-start = (bf16[2,48,4096]{2,1,0:T(8,128)(2,1)}, bf16[2,48,4096]{2,1,0:T(8,128)(2,1)}, u32[]{:S(2)}, u32[]{:S(2)}) collective-permute-start(bf16[2,48,4096]{2,1,0:T(8,128)(2,1)} %refs_5_.3), channel_id=1, source_target_pairs={{0,2},{1,3},{2,0},{3,1},{4,6},{5,7},{6,4},{7,5},{8,10},{9,11},{10,... | collective-permute-start | bytes 2359304 | tf_op jit(solution)/shard_map/ppermute | solution.py:241
  2.9 1.5 %collective-permute-start.1 = (bf16[2,48,4096]{2,1,0:T(8,128)(2,1)}, bf16[2,48,4096]{2,1,0:T(8,128)(2,1)}, u32[]{:S(2)}, u32[]{:S(2)}) collective-permute-start(bf16[2,48,4096]{2,1,0:T(8,128)(2,1)} %refs_5_.3), channel_id=1, source_target_pairs={{0,4},{1,5},{2,6},{3,7},{4,0},{5,1},{6,2},{7,3},{8,12},{9,13},{10,... | collective-permute-start | bytes 2359304 | tf_op jit(solution)/shard_map/ppermute | solution.py:241
  4.5 1.9 %fusion.8 = (bf16[2,96,1024]{2,1,0:T(8,128)(2,1)}, bf16[2,96,1024]{2,1,0:T(8,128)(2,1)S(1)}) fusion(bf16[2,96,2048]{2,1,0:T(8,128)(2,1)} %param.5), kind=kLoop, calls=%fused_computation.21 | loop fusion | bytes 1572864 | tf_op jit(solution)/shard_map/slice | solution.py:283
  6.4 3.6 %collective-permute-start.2 = (bf16[2,96,1024]{2,1,0:T(8,128)(2,1)S(1)}, bf16[2,96,1024]{2,1,0:T(8,128)(2,1)}, u32[]{:S(2)}, u32[]{:S(2)}) collective-permute-start(bf16[2,96,1024]{2,1,0:T(8,128)(2,1)S(1)} %get-tuple-element.20.refs_1_), channel_id=1, source_target_pairs={{0,24},{8,16},{16,8},{24,0},{1,25},{9,17},{17,9},{25,1},{2,26},{10... | collective-permute-start | bytes 1179656 | tf_op jit(solution)/shard_map/ppermute | solution.py:241
  10.0 7.3 %shard_map.47.refs_16_ = bf16[2048,768]{1,0:T(8,128)(2,1)} custom-call(f32[2048,384]{1,0:T(8,128)} %phase_ref.3), custom_call_target="tpu_custom_call" | custom-call | flops 7864 | bytes 7864 | tf_op jit(solution)/shard_map/pallas_call | solution.py:46
  17.3 10.9 %shard_map.46.refs_15_ = bf16[3,384,4096]{2,1,0:T(8,128)(2,1)} custom-call(f32[4096,384]{1,0:T(8,128)} %phase_ref.2), custom_call_target="tpu_custom_call" | custom-call | flops 15728 | bytes 15728 | tf_op jit(solution)/shard_map/pallas_call | solution.py:46
  28.8 1.0 slice.38
  32.1 1.6 %collective-permute-start.4 = (bf16[2,96,1024]{2,1,0:T(8,128)(2,1)S(1)}, bf16[2,96,1024]{2,1,0:T(8,128)(2,1)S(1)}, u32[]{:S(2)}, u32[]{:S(2)}) collective-permute-start(bf16[2,96,1024]{2,1,0:T(8,128)(2,1)S(1)} %broadcast_select_fusion), channel_id=1, source_target_pairs={{8,0},{16,24},{0,16},{24,8},{9,1},{17,25},{1,17},{25,9},{10,2},{18... | collective-permute-start | bytes 1179656 | tf_op jit(solution)/shard_map/ppermute | solution.py:295
  33.7 6.2 %collective-permute-done.11.refs_11_ = bf16[1,48,4096]{2,1,0:T(8,128)(2,1)S(1)} collective-permute-done((bf16[1,48,4096]{2,1,0:T(8,128)(2,1)S(1)}, bf16[1,48,4096]{2,1,0:T(8,128)(2,1)S(1)}, u32[]{:S(2)}, u32[]{:S(2)}) %collective-permute-start.11) | collective-permute-done | bytes 393248 | tf_op jit(solution)/shard_map/ppermute | solution.py:241
  39.9 3.1 %collective-permute-done.12.refs_12_ = bf16[1,48,4096]{2,1,0:T(8,128)(2,1)S(1)} collective-permute-done((bf16[1,48,4096]{2,1,0:T(8,128)(2,1)S(1)}, bf16[1,48,4096]{2,1,0:T(8,128)(2,1)S(1)}, u32[]{:S(2)}, u32[]{:S(2)}) %collective-permute-start.12) | collective-permute-done | bytes 393248 | tf_op jit(solution)/shard_map/ppermute | solution.py:241
  43.1 1.6 %collective-permute-done.4.refs_3_ = bf16[2,96,1024]{2,1,0:T(8,128)(2,1)S(1)} collective-permute-done((bf16[2,96,1024]{2,1,0:T(8,128)(2,1)S(1)}, bf16[2,96,1024]{2,1,0:T(8,128)(2,1)S(1)}, u32[]{:S(2)}, u32[]{:S(2)}) %collective-permute-start.4) | collective-permute-done | bytes 393248 | tf_op jit(solution)/shard_map/ppermute | solution.py:295
  44.7 2.7 %collective-permute-start.5 = (bf16[2,96,1024]{2,1,0:T(8,128)(2,1)}, bf16[2,96,1024]{2,1,0:T(8,128)(2,1)}, u32[]{:S(2)}, u32[]{:S(2)}) collective-permute-start(bf16[2,96,1024]{2,1,0:T(8,128)(2,1)} %get-tuple-element.22.refs_1_), channel_id=1, source_target_pairs={{0,8},{8,0},{16,24},{24,16},{1,9},{9,1},{17,25},{25,17},{2,10},{10... | collective-permute-start | bytes 1179656 | tf_op jit(solution)/shard_map/ppermute | solution.py:241
  47.5 2.4 %collective-permute-start.7 = (bf16[2,96,1024]{2,1,0:T(8,128)(2,1)}, bf16[2,96,1024]{2,1,0:T(8,128)(2,1)}, u32[]{:S(2)}, u32[]{:S(2)}) collective-permute-start(bf16[2,96,1024]{2,1,0:T(8,128)(2,1)} %get-tuple-element.22.refs_1_), channel_id=1, source_target_pairs={{0,24},{8,16},{16,8},{24,0},{1,25},{9,17},{17,9},{25,1},{2,26},{10... | collective-permute-start | bytes 1179656 | tf_op jit(solution)/shard_map/ppermute | solution.py:241
  50.0 28.6 %shard_map.48.refs_17_ = f32[384,768]{1,0:T(8,128)} custom-call(s32[9]{0:T(128)} %stack.39.refs_0_, bf16[2,96,1024]{2,1,0:T(8,128)(2,1)} %copy-done, bf16[2,96,1024]{2,1,0:T(8,128)(2,1)} %collective-permute-done.3.refs_2_, bf16[2,96,1024]{2,1,0:T(8,128)(2,1)} %copy-done.4, bf16[2,96,1024]{2,1,0:T(8,128)(2,1)} %collective-permute-done.2.refs_4_, ...), custom_call_target="tpu_custom_call" | custom-call | flops 20401094656 | bytes 16777216 | tf_op jit(solution)/shard_map/pallas_call | solution.py:217
  78.6 29.3 %shard_map.49 = (bf16[4,96,384]{2,1,0:T(8,128)(2,1)}, bf16[4,96,384]{2,1,0:T(8,128)(2,1)}) custom-call(s32[9]{0:T(128)} %stack.39.refs_0_, bf16[2,96,1024]{2,1,0:T(8,128)(2,1)} %get-tuple-element.22.refs_1_, bf16[2,96,1024]{2,1,0:T(8,128)(2,1)} %collective-permute-done.5.refs_2_, bf16[2,96,1024]{2,1,0:T(8,128)(2,1)} %collective-permute-done.6.refs_3_, ...), custom_call_target="tpu_custom_call" | custom-call | flops 20401094656 | bytes 16777216 | tf_op jit(solution)/shard_map/pallas_call | solution.py:217
  107.9 1.8 %collective-permute-done.15 = bf16[4,96,384]{2,1,0:T(8,128)(2,1)S(1)} collective-permute-done((bf16[4,96,384]{2,1,0:T(8,128)(2,1)}, bf16[4,96,384]{2,1,0:T(8,128)(2,1)S(1)}, u32[]{:S(2)}, u32[]{:S(2)}) %collective-permute-start.15) | collective-permute-done | bytes 294944 | tf_op jit(solution)/shard_map/ppermute | solution.py:241
  110.7 1.6 %collective-permute-start.16 = (bf16[96,384]{1,0:T(8,128)(2,1)S(1)}, bf16[96,384]{1,0:T(8,128)(2,1)S(1)}, u32[]{:S(2)}, u32[]{:S(2)}) collective-permute-start(bf16[96,384]{1,0:T(8,128)(2,1)S(1)} %get-tuple-element.33), channel_id=1, source_target_pairs={{0,2},{1,3},{2,0},{3,1},{4,6},{5,7},{6,4},{7,5},{8,10},{9,11},{10,... | collective-permute-start | bytes 221192 | tf_op jit(solution)/shard_map/ppermute | solution.py:241
  112.3 1.5 %collective-permute-start.17 = (bf16[96,384]{1,0:T(8,128)(2,1)S(1)}, bf16[96,384]{1,0:T(8,128)(2,1)S(1)}, u32[]{:S(2)}, u32[]{:S(2)}) collective-permute-start(bf16[96,384]{1,0:T(8,128)(2,1)S(1)} %get-tuple-element.35), channel_id=1, source_target_pairs={{0,4},{1,5},{2,6},{3,7},{4,0},{5,1},{6,2},{7,3},{8,12},{9,13},{10,... | collective-permute-start | bytes 221192 | tf_op jit(solution)/shard_map/ppermute | solution.py:241
  115.2 1.5 %collective-permute-done.17 = bf16[96,384]{1,0:T(8,128)(2,1)S(1)} collective-permute-done((bf16[96,384]{1,0:T(8,128)(2,1)S(1)}, bf16[96,384]{1,0:T(8,128)(2,1)S(1)}, u32[]{:S(2)}, u32[]{:S(2)}) %collective-permute-start.17) | collective-permute-done | bytes 73760 | tf_op jit(solution)/shard_map/ppermute | solution.py:241
  116.6 2.4 %collective-permute-done.18 = bf16[96,384]{1,0:T(8,128)(2,1)S(1)} collective-permute-done((bf16[96,384]{1,0:T(8,128)(2,1)S(1)}, bf16[96,384]{1,0:T(8,128)(2,1)S(1)}, u32[]{:S(2)}, u32[]{:S(2)}) %collective-permute-start.18) | collective-permute-done | bytes 73760 | tf_op jit(solution)/shard_map/ppermute | solution.py:241
  120.4 7.3 %collective-permute-start.19 = (bf16[96,96]{1,0:T(8,128)(2,1)S(1)}, bf16[96,96]{1,0:T(8,128)(2,1)S(1)}, u32[]{:S(2)}, u32[]{:S(2)}) collective-permute-start(bf16[96,96]{1,0:T(8,128)(2,1)S(1)} %bitcast.43), channel_id=1, source_target_pairs={{0,8},{8,0},{16,24},{24,16},{1,9},{9,1},{17,25},{25,17},{2,10},{10... | collective-permute-start | bytes 55304 | tf_op jit(solution)/shard_map/ppermute | solution.py:241
  128.0 2.4 %collective-permute-start.21 = (bf16[96,96]{1,0:T(8,128)(2,1)S(1)}, bf16[96,96]{1,0:T(8,128)(2,1)S(1)}, u32[]{:S(2)}, u32[]{:S(2)}) collective-permute-start(bf16[96,96]{1,0:T(8,128)(2,1)S(1)} %bitcast.45), channel_id=1, source_target_pairs={{0,24},{8,16},{16,8},{24,0},{1,25},{9,17},{17,9},{25,1},{2,26},{10... | collective-permute-start | bytes 55304 | tf_op jit(solution)/shard_map/ppermute | solution.py:241
  130.5 2.0 %collective-permute-done.20 = bf16[96,96]{1,0:T(8,128)(2,1)S(1)} collective-permute-done((bf16[96,96]{1,0:T(8,128)(2,1)S(1)}, bf16[96,96]{1,0:T(8,128)(2,1)S(1)}, u32[]{:S(2)}, u32[]{:S(2)}) %collective-permute-start.20) | collective-permute-done | bytes 18464 | tf_op jit(solution)/shard_map/ppermute | solution.py:241
  132.6 1.1 collective-permute-done.21
  (52 shorter events, 7.9 us)
Async XLA Ops:
  0.0 28.8 %collective-permute-start = (bf16[2,48,4096]{2,1,0:T(8,128)(2,1)}, bf16[2,48,4096]{2,1,0:T(8,128)(2,1)}, u32[]{:S(2)}, u32[]{:S(2)}) collective-permute-start(bf16[2,48,4096]{2,1,0:T(8,128)(2,1)} %refs_5_.3), channel_id=1, source_target_pairs={{0,2},{1,3},{2,0},{3,1},{4,6},{5,7},{6,4},{7,5},{8,10},{9,11},{10,... | collective-permute-start | bytes 2359304 | tf_op jit(solution)/shard_map/ppermute | solution.py:241
  2.9 25.9 %collective-permute-start.1 = (bf16[2,48,4096]{2,1,0:T(8,128)(2,1)}, bf16[2,48,4096]{2,1,0:T(8,128)(2,1)}, u32[]{:S(2)}, u32[]{:S(2)}) collective-permute-start(bf16[2,48,4096]{2,1,0:T(8,128)(2,1)} %refs_5_.3), channel_id=1, source_target_pairs={{0,4},{1,5},{2,6},{3,7},{4,0},{5,1},{6,2},{7,3},{8,12},{9,13},{10,... | collective-permute-start | bytes 2359304 | tf_op jit(solution)/shard_map/ppermute | solution.py:241
  6.4 25.7 %copy-start = (bf16[2,96,1024]{2,1,0:T(8,128)(2,1)}, bf16[2,96,1024]{2,1,0:T(8,128)(2,1)S(1)}, u32[]{:S(2)}) copy-start(bf16[2,96,1024]{2,1,0:T(8,128)(2,1)S(1)} %get-tuple-element.20.refs_1_) | copy-start | bytes 1179652
  6.4 22.4 %collective-permute-start.2 = (bf16[2,96,1024]{2,1,0:T(8,128)(2,1)S(1)}, bf16[2,96,1024]{2,1,0:T(8,128)(2,1)}, u32[]{:S(2)}, u32[]{:S(2)}) collective-permute-start(bf16[2,96,1024]{2,1,0:T(8,128)(2,1)S(1)} %get-tuple-element.20.refs_1_), channel_id=1, source_target_pairs={{0,24},{8,16},{16,8},{24,0},{1,25},{9,17},{17,9},{25,1},{2,26},{10... | collective-permute-start | bytes 1179656 | tf_op jit(solution)/shard_map/ppermute | solution.py:241
  10.0 18.8 %collective-permute-start.3 = (bf16[2,96,1024]{2,1,0:T(8,128)(2,1)S(1)}, bf16[2,96,1024]{2,1,0:T(8,128)(2,1)}, u32[]{:S(2)}, u32[]{:S(2)}) collective-permute-start(bf16[2,96,1024]{2,1,0:T(8,128)(2,1)S(1)} %get-tuple-element.20.refs_1_), channel_id=1, source_target_pairs={{0,8},{8,0},{16,24},{24,16},{1,9},{9,1},{17,25},{25,17},{2,10},{10... | collective-permute-start | bytes 1179656 | tf_op jit(solution)/shard_map/ppermute | solution.py:241
  29.9 10.1 %collective-permute-start.11 = (bf16[1,48,4096]{2,1,0:T(8,128)(2,1)S(1)}, bf16[1,48,4096]{2,1,0:T(8,128)(2,1)S(1)}, u32[]{:S(2)}, u32[]{:S(2)}) collective-permute-start(bf16[1,48,4096]{2,1,0:T(8,128)(2,1)S(1)} %slice.38), channel_id=1, source_target_pairs={{0,2},{1,3},{2,0},{3,1},{4,6},{5,7},{6,4},{7,5},{8,10},{9,11},{10,... | collective-permute-start | bytes 1179656 | tf_op jit(solution)/shard_map/ppermute | solution.py:241
  30.5 14.2 %collective-permute-start.8 = (bf16[2,48,4096]{2,1,0:T(8,128)(2,1)}, bf16[2,48,4096]{2,1,0:T(8,128)(2,1)}, u32[]{:S(2)}, u32[]{:S(2)}) collective-permute-start(bf16[2,48,4096]{2,1,0:T(8,128)(2,1)} %refs_5_.3), channel_id=1, source_target_pairs={{0,1},{1,0},{2,3},{3,2},{4,5},{5,4},{6,7},{7,6},{8,9},{9,8},{10,11... | collective-permute-start | bytes 2359304 | tf_op jit(solution)/shard_map/ppermute | solution.py:241
  31.5 11.6 %collective-permute-start.12 = (bf16[1,48,4096]{2,1,0:T(8,128)(2,1)S(1)}, bf16[1,48,4096]{2,1,0:T(8,128)(2,1)S(1)}, u32[]{:S(2)}, u32[]{:S(2)}) collective-permute-start(bf16[1,48,4096]{2,1,0:T(8,128)(2,1)S(1)} %slice.39), channel_id=1, source_target_pairs={{0,4},{1,5},{2,6},{3,7},{4,0},{5,1},{6,2},{7,3},{8,12},{9,13},{10,... | collective-permute-start | bytes 1179656 | tf_op jit(solution)/shard_map/ppermute | solution.py:241
  32.1 12.6 %collective-permute-start.4 = (bf16[2,96,1024]{2,1,0:T(8,128)(2,1)S(1)}, bf16[2,96,1024]{2,1,0:T(8,128)(2,1)S(1)}, u32[]{:S(2)}, u32[]{:S(2)}) collective-permute-start(bf16[2,96,1024]{2,1,0:T(8,128)(2,1)S(1)} %broadcast_select_fusion), channel_id=1, source_target_pairs={{8,0},{16,24},{0,16},{24,8},{9,1},{17,25},{1,17},{25,9},{10,2},{18... | collective-permute-start | bytes 1179656 | tf_op jit(solution)/shard_map/ppermute | solution.py:295
  33.7 16.2 %collective-permute-start.10 = (bf16[2,48,4096]{2,1,0:T(8,128)(2,1)}, bf16[2,48,4096]{2,1,0:T(8,128)(2,1)}, u32[]{:S(2)}, u32[]{:S(2)}) collective-permute-start(bf16[2,48,4096]{2,1,0:T(8,128)(2,1)} %collective-permute-done.1.refs_7_), channel_id=1, source_target_pairs={{0,1},{1,0},{2,3},{3,2},{4,5},{5,4},{6,7},{7,6},{8,9},{9,8},{10,11... | collective-permute-start | bytes 2359304 | tf_op jit(solution)/shard_map/ppermute | solution.py:241
  39.9 4.8 %copy-start.1 = (bf16[1,48,4096]{2,1,0:T(8,128)(2,1)}, bf16[1,48,4096]{2,1,0:T(8,128)(2,1)S(1)}, u32[]{:S(2)}) copy-start(bf16[1,48,4096]{2,1,0:T(8,128)(2,1)S(1)} %collective-permute-done.11.refs_11_) | copy-start | bytes 1179652
  39.9 10.0 %collective-permute-start.9 = (bf16[2,48,4096]{2,1,0:T(8,128)(2,1)}, bf16[2,48,4096]{2,1,0:T(8,128)(2,1)}, u32[]{:S(2)}, u32[]{:S(2)}) collective-permute-start(bf16[2,48,4096]{2,1,0:T(8,128)(2,1)} %collective-permute-done.refs_6_), channel_id=1, source_target_pairs={{0,1},{1,0},{2,3},{3,2},{4,5},{5,4},{6,7},{7,6},{8,9},{9,8},{10,11... | collective-permute-start | bytes 2359304 | tf_op jit(solution)/shard_map/ppermute | solution.py:241
  43.1 4.3 %collective-permute-start.13 = (bf16[1,48,4096]{2,1,0:T(8,128)(2,1)S(1)}, bf16[1,48,4096]{2,1,0:T(8,128)(2,1)S(1)}, u32[]{:S(2)}, u32[]{:S(2)}) collective-permute-start(bf16[1,48,4096]{2,1,0:T(8,128)(2,1)S(1)} %collective-permute-done.11.refs_11_), channel_id=1, source_target_pairs={{0,1},{1,0},{2,3},{3,2},{4,5},{5,4},{6,7},{7,6},{8,9},{9,8},{10,11... | collective-permute-start | bytes 1179656 | tf_op jit(solution)/shard_map/ppermute | solution.py:241
  44.7 2.8 %collective-permute-start.14 = (bf16[1,48,4096]{2,1,0:T(8,128)(2,1)S(1)}, bf16[1,48,4096]{2,1,0:T(8,128)(2,1)S(1)}, u32[]{:S(2)}, u32[]{:S(2)}) collective-permute-start(bf16[1,48,4096]{2,1,0:T(8,128)(2,1)S(1)} %collective-permute-done.12.refs_12_), channel_id=1, source_target_pairs={{0,1},{1,0},{2,3},{3,2},{4,5},{5,4},{6,7},{7,6},{8,9},{9,8},{10,11... | collective-permute-start | bytes 1179656 | tf_op jit(solution)/shard_map/ppermute | solution.py:241
  44.7 33.8 %collective-permute-start.5 = (bf16[2,96,1024]{2,1,0:T(8,128)(2,1)}, bf16[2,96,1024]{2,1,0:T(8,128)(2,1)}, u32[]{:S(2)}, u32[]{:S(2)}) collective-permute-start(bf16[2,96,1024]{2,1,0:T(8,128)(2,1)} %get-tuple-element.22.refs_1_), channel_id=1, source_target_pairs={{0,8},{8,0},{16,24},{24,16},{1,9},{9,1},{17,25},{25,17},{2,10},{10... | collective-permute-start | bytes 1179656 | tf_op jit(solution)/shard_map/ppermute | solution.py:241
  47.4 31.1 %collective-permute-start.6 = (bf16[2,96,1024]{2,1,0:T(8,128)(2,1)}, bf16[2,96,1024]{2,1,0:T(8,128)(2,1)}, u32[]{:S(2)}, u32[]{:S(2)}) collective-permute-start(bf16[2,96,1024]{2,1,0:T(8,128)(2,1)} %get-tuple-element.22.refs_1_), channel_id=1, source_target_pairs={{0,16},{8,24},{16,0},{24,8},{1,17},{9,25},{17,1},{25,9},{2,18},{10... | collective-permute-start | bytes 1179656 | tf_op jit(solution)/shard_map/ppermute | solution.py:241
  47.5 31.0 %collective-permute-start.7 = (bf16[2,96,1024]{2,1,0:T(8,128)(2,1)}, bf16[2,96,1024]{2,1,0:T(8,128)(2,1)}, u32[]{:S(2)}, u32[]{:S(2)}) collective-permute-start(bf16[2,96,1024]{2,1,0:T(8,128)(2,1)} %get-tuple-element.22.refs_1_), channel_id=1, source_target_pairs={{0,24},{8,16},{16,8},{24,0},{1,25},{9,17},{17,9},{25,1},{2,26},{10... | collective-permute-start | bytes 1179656 | tf_op jit(solution)/shard_map/ppermute | solution.py:241
  107.9 1.9 %collective-permute-start.15 = (bf16[4,96,384]{2,1,0:T(8,128)(2,1)}, bf16[4,96,384]{2,1,0:T(8,128)(2,1)S(1)}, u32[]{:S(2)}, u32[]{:S(2)}) collective-permute-start(bf16[4,96,384]{2,1,0:T(8,128)(2,1)} %get-tuple-element.30), channel_id=1, source_target_pairs={{0,1},{1,0},{2,3},{3,2},{4,5},{5,4},{6,7},{7,6},{8,9},{9,8},{10,11... | collective-permute-start | bytes 884744 | tf_op jit(solution)/shard_map/ppermute | solution.py:241
  110.7 4.4 %collective-permute-start.16 = (bf16[96,384]{1,0:T(8,128)(2,1)S(1)}, bf16[96,384]{1,0:T(8,128)(2,1)S(1)}, u32[]{:S(2)}, u32[]{:S(2)}) collective-permute-start(bf16[96,384]{1,0:T(8,128)(2,1)S(1)} %get-tuple-element.33), channel_id=1, source_target_pairs={{0,2},{1,3},{2,0},{3,1},{4,6},{5,7},{6,4},{7,5},{8,10},{9,11},{10,... | collective-permute-start | bytes 221192 | tf_op jit(solution)/shard_map/ppermute | solution.py:241
  112.3 4.4 %collective-permute-start.17 = (bf16[96,384]{1,0:T(8,128)(2,1)S(1)}, bf16[96,384]{1,0:T(8,128)(2,1)S(1)}, u32[]{:S(2)}, u32[]{:S(2)}) collective-permute-start(bf16[96,384]{1,0:T(8,128)(2,1)S(1)} %get-tuple-element.35), channel_id=1, source_target_pairs={{0,4},{1,5},{2,6},{3,7},{4,0},{5,1},{6,2},{7,3},{8,12},{9,13},{10,... | collective-permute-start | bytes 221192 | tf_op jit(solution)/shard_map/ppermute | solution.py:241
  113.8 5.3 %collective-permute-start.18 = (bf16[96,384]{1,0:T(8,128)(2,1)S(1)}, bf16[96,384]{1,0:T(8,128)(2,1)S(1)}, u32[]{:S(2)}, u32[]{:S(2)}) collective-permute-start(bf16[96,384]{1,0:T(8,128)(2,1)S(1)} %get-tuple-element.34), channel_id=1, source_target_pairs={{0,6},{1,7},{2,4},{3,5},{4,2},{5,3},{6,0},{7,1},{8,14},{9,15},{10,... | collective-permute-start | bytes 221192 | tf_op jit(solution)/shard_map/ppermute | solution.py:241
  120.4 10.1 %collective-permute-start.19 = (bf16[96,96]{1,0:T(8,128)(2,1)S(1)}, bf16[96,96]{1,0:T(8,128)(2,1)S(1)}, u32[]{:S(2)}, u32[]{:S(2)}) collective-permute-start(bf16[96,96]{1,0:T(8,128)(2,1)S(1)} %bitcast.43), channel_id=1, source_target_pairs={{0,8},{8,0},{16,24},{24,16},{1,9},{9,1},{17,25},{25,17},{2,10},{10... | collective-permute-start | bytes 55304 | tf_op jit(solution)/shard_map/ppermute | solution.py:241
  127.8 4.8 %collective-permute-start.20 = (bf16[96,96]{1,0:T(8,128)(2,1)S(1)}, bf16[96,96]{1,0:T(8,128)(2,1)S(1)}, u32[]{:S(2)}, u32[]{:S(2)}) collective-permute-start(bf16[96,96]{1,0:T(8,128)(2,1)S(1)} %bitcast.44), channel_id=1, source_target_pairs={{0,16},{8,24},{16,0},{24,8},{1,17},{9,25},{17,1},{25,9},{2,18},{10... | collective-permute-start | bytes 55304 | tf_op jit(solution)/shard_map/ppermute | solution.py:241
  128.0 5.7 %collective-permute-start.21 = (bf16[96,96]{1,0:T(8,128)(2,1)S(1)}, bf16[96,96]{1,0:T(8,128)(2,1)S(1)}, u32[]{:S(2)}, u32[]{:S(2)}) collective-permute-start(bf16[96,96]{1,0:T(8,128)(2,1)S(1)} %bitcast.45), channel_id=1, source_target_pairs={{0,24},{8,16},{16,8},{24,0},{1,25},{9,17},{17,9},{25,1},{2,26},{10... | collective-permute-start | bytes 55304 | tf_op jit(solution)/shard_map/ppermute | solution.py:241
  (4 other events, 12.1 us)
